TPU v7x, 256 devices: a whole 4x4x8 slice. The times are simulated.
256 devices in a mesh: gx: 16 (over z, core), gy: 4 (over x), gz: 4 (over y).
Axes of the slice: x: 4, y: 4, z: 8, core: 2. Of those that a mesh axis runs over, the one named last changes fastest.
Arguments:
- heights: float32 [8192, 8192], P(('gy', 'gz'), 'gx'), may hold values from -6 to 6
- scene_ids: int32 [8192, 8192], P(('gy', 'gz'), 'gx'), may hold values from 0 to 15, as said below
- scene_offset: float32 [16], replicated, may hold values from -4 to 4
- scene_weight: float32 [16], replicated, may hold values from 0.2 to 5
- band_gain: float32 [6], replicated, may hold values from 0.3 to 1.5
Outputs:
- blended: float32 [8192, 8192], P(('gy', 'gz'), 'gx')
Inputs may be any that keep to these rules, and one draw needn't show every extreme that they name: `scene_ids`: scene index of each cell.
All inputs are finite; a program needn't handle non-finite values.
Results may differ from a plain program's by a relative error of at most 0.00002.
Values sent between devices are 32-bit elements; how exact they have to be, the bound alone decides.
No kernel may reach another device: no remote copies, remote signals or barrier semaphores. Data moves between devices by JAX's collectives and lax.ppermute only.
A program may use at most 128 MiB of HBM per device.

v0:
```python
import jax
import jax.numpy as jnp
from jax import lax
from jax.sharding import Mesh
from jax.sharding import PartitionSpec as P

SCENES = 16
LEVELS = 6
GX_GY_GZ = ("gx_0", "gx_1", "gy", "gz")
GX = ("gx_0", "gx_1")


KERN = (0.0625, 0.25, 0.375, 0.25, 0.0625)


def extended(block, sides, width):
    for axis, dim in sides:
        count = lax.axis_size(axis)
        forward = [(i, i + 1) for i in range(count - 1)]
        backward = [(target, source) for source, target in forward]
        low = lax.ppermute(
            lax.slice_in_dim(block, block.shape[dim] - width, None, axis=dim), axis, forward
        )
        high = lax.ppermute(lax.slice_in_dim(block, 0, width, axis=dim), axis, backward)
        block = jnp.concatenate([low, block, high], axis=dim)
    return block


def over_axes(x, axes):
    for axis in axes:
        x = lax.psum(x, axis)
    return x


def lookup(scene_ids, table):
    acc = jnp.zeros(scene_ids.shape, jnp.float32)
    for scene in range(SCENES):
        acc = acc + jnp.where(scene_ids == scene, table[scene], jnp.float32(0.0))
    return acc


def reduce_padded(padded):
    rows_out = padded.shape[-2] - 4
    cols_out = padded.shape[-1] - 4
    rows = KERN[0] * padded[..., 0:rows_out:2, :]
    for tap in range(1, 5):
        rows = rows + KERN[tap] * padded[..., tap : tap + rows_out : 2, :]
    result = KERN[0] * rows[..., 0:cols_out:2]
    for tap in range(1, 5):
        result = result + KERN[tap] * rows[..., tap : tap + cols_out : 2]
    return result


def expand_padded(padded):
    count = padded.shape[-2] - 2
    even = (
        padded[..., 0:count, :]
        + 6.0 * padded[..., 1 : count + 1, :]
        + padded[..., 2 : count + 2, :]
    ) * 0.125
    odd = (padded[..., 1 : count + 1, :] + padded[..., 2 : count + 2, :]) * 0.5
    rows = jnp.stack([even, odd], axis=-2)
    rows = rows.reshape(rows.shape[:-3] + (2 * count, rows.shape[-1]))
    width = rows.shape[-1] - 2
    even = (rows[..., 0:width] + 6.0 * rows[..., 1 : width + 1] + rows[..., 2 : width + 2]) * 0.125
    odd = (rows[..., 1 : width + 1] + rows[..., 2 : width + 2]) * 0.5
    result = jnp.stack([even, odd], axis=-1)
    return result.reshape(result.shape[:-2] + (2 * width,))


def reduce_level(pair):
    rimmed = extended(pair, ((GX, 2), (("gy", "gz"), 1)), 2)
    return reduce_padded(rimmed)


def rim_up(stacked):
    return extended(stacked, ((GX, 2), (("gy", "gz"), 1)), 1)


def local(heights, scene_ids, scene_offset, scene_weight, band_gain):
    weight = lookup(scene_ids, scene_weight)
    offset = lookup(scene_ids, scene_offset)
    pair = jnp.stack([weight * (heights + offset), weight])
    ratios = [pair[0] / pair[1]]
    tile_levels = LEVELS
    for level in range(tile_levels):
        pair = reduce_level(pair)
        ratios.append(pair[0] / pair[1])
    top_ratio = ratios[LEVELS]
    total_num, total_den = (
        over_axes(jnp.sum(pair[0]), GX_GY_GZ),
        over_axes(jnp.sum(pair[1]), GX_GY_GZ),
    )
    top_field = jnp.zeros_like(top_ratio) + total_num / total_den
    piece = rim_up(jnp.stack([top_ratio, top_field]))
    for level in range(LEVELS - 1, -1, -1):
        expanded = expand_padded(piece)
        blended = band_gain[level] * (ratios[level] - expanded[0]) + expanded[1]
        if level > 0:
            piece = rim_up(jnp.stack([ratios[level], blended]))
    return blended


def solution(mesh):
    torus = Mesh(
        mesh.devices.reshape(8, 2, mesh.shape["gy"], mesh.shape["gz"]), ("gx_0", "gx_1", "gy", "gz")
    )
    placed = (P(("gy", "gz"), GX), P(("gy", "gz"), GX), P(), P(), P())
    return jax.shard_map(
        local, mesh=torus, in_specs=placed, out_specs=P(("gy", "gz"), GX), check_vma=False
    )
```

profile of v0, /device:TPU:130, one launch (start us, length us, event | category | flops | bytes accessed | tf_op | source)
XLA Modules:
  0.0 613.7 jit_solution(1630181600630466397)
XLA Ops:
  6.2 23.3 %add_multiply_fusion = (f32[512,512]{0,1:T(8,128)S(1)}, f32[512,512]{0,1:T(8,128)S(1)}) fusion(f32[512,512]{0,1:T(8,128)S(1)} %copy.132, pred[512,512]{0,1:T(8,128)(4,1)S(1)} %get-tuple-element.39, pred[512,512]{0,1:T(8,128)(4,1)S(1)} %get-tuple-element.40, pred[512,512]{0,1:T(8,128)(4,1)S(1)} %get-tuple-element.41, ...), kind=kLoop, calls=%fused_computation.14 | loop fusion | flops 16777216 | bytes 7340160 | tf_op jit(solution)/shard_map/mul | solution.py:83
  39.6 4.9 collective-permute-start.3
  46.9 39.8 %slice.683 = f32[2,256,516]{1,2,0:T(8,128)} slice(f32[2,512,516]{1,2,0:T(8,128)} %copy-done), slice={[0:2:1], [0:512:2], [0:516:1]} | slice | bytes 2113536 | tf_op jit(solution)/shard_map/slice | solution.py:47
  89.7 39.9 %slice.685 = f32[2,256,516]{1,2,0:T(8,128)} slice(f32[2,516,516]{1,2,0:T(8,128)} %pad_maximum_fusion), slice={[0:2:1], [4:516:2], [0:516:1]} | slice | bytes 2113536 | tf_op jit(solution)/shard_map/slice | solution.py:47
  129.6 39.9 %slice.684 = f32[2,256,516]{1,2,0:T(8,128)} slice(f32[2,516,516]{1,2,0:T(8,128)} %pad_maximum_fusion), slice={[0:2:1], [3:515:2], [0:516:1]} | slice | bytes 2113536 | tf_op jit(solution)/shard_map/slice | solution.py:47
  169.5 40.1 %slice.682 = f32[2,256,516]{1,2,0:T(8,128)} slice(f32[2,516,516]{1,2,0:T(8,128)} %pad_maximum_fusion), slice={[0:2:1], [1:513:2], [0:516:1]} | slice | bytes 2113536 | tf_op jit(solution)/shard_map/slice | solution.py:47
  209.6 39.8 %slice.681 = f32[2,256,516]{1,2,0:T(8,128)} slice(f32[2,516,516]{1,2,0:T(8,128)} %pad_maximum_fusion), slice={[0:2:1], [0:512:2], [0:516:1]} | slice | bytes 2113536 | tf_op jit(solution)/shard_map/slice | solution.py:45
  274.1 6.0 collective-permute-start.7
  282.0 10.5 %slice.700 = f32[2,128,260]{1,2,0:T(8,128)} slice(f32[2,256,260]{1,2,0:T(8,128)S(1)} %pad_maximum_fusion.13), slice={[0:2:1], [0:256:2], [0:260:1]} | slice | bytes 532480 | tf_op jit(solution)/shard_map/slice | solution.py:47
  294.6 10.1 %slice.702 = f32[2,128,260]{1,2,0:T(8,128)} slice(f32[2,260,260]{1,2,0:T(8,128)S(1)} %pad_maximum_fusion.4), slice={[0:2:1], [4:260:2], [0:260:1]} | slice | bytes 532480 | tf_op jit(solution)/shard_map/slice | solution.py:47
  304.7 10.0 %slice.701 = f32[2,128,260]{1,2,0:T(8,128)} slice(f32[2,260,260]{1,2,0:T(8,128)S(1)} %pad_maximum_fusion.4), slice={[0:2:1], [3:259:2], [0:260:1]} | slice | bytes 532480 | tf_op jit(solution)/shard_map/slice | solution.py:47
  314.7 10.1 %slice.699 = f32[2,128,260]{1,2,0:T(8,128)} slice(f32[2,260,260]{1,2,0:T(8,128)S(1)} %pad_maximum_fusion.4), slice={[0:2:1], [1:257:2], [0:260:1]} | slice | bytes 532480 | tf_op jit(solution)/shard_map/slice | solution.py:47
  324.9 10.0 %slice.698 = f32[2,128,260]{1,2,0:T(8,128)} slice(f32[2,260,260]{1,2,0:T(8,128)S(1)} %pad_maximum_fusion.4), slice={[0:2:1], [0:256:2], [0:260:1]} | slice | bytes 532480 | tf_op jit(solution)/shard_map/slice | solution.py:45
  346.8 6.0 collective-permute-start.11
  357.2 4.6 collective-permute-done.10
  383.8 4.2 collective-permute-start.14
  433.6 14.8 %all-reduce.1 = (f32[]{:T(128)}, f32[]{:T(128)}) all-reduce(f32[]{:T(128)} %get-tuple-element.6, f32[]{:T(128)} %get-tuple-element.5), channel_id=1, replica_groups=mesh['gx_0'=8,'gx_1'=2,'gy'=4,'gz'=4] {'gx_0'}, use_global_device_ids=true, to_apply=%region_1.2 | all-reduce | flops 2 | bytes 16 | tf_op jit(solution)/shard_map/psum | solution.py:31
  451.5 9.3 %all-reduce.3 = (f32[]{:T(128)}, f32[]{:T(128)}) all-reduce(f32[]{:T(128)} %get-tuple-element.13, f32[]{:T(128)} %get-tuple-element.14), channel_id=1, replica_groups=mesh['gx_0'=8,'gx_1'=2,'gy'=4,'gz'=4] {'gy'}, use_global_device_ids=true, to_apply=%region_3.4 | all-reduce | flops 2 | bytes 16 | tf_op jit(solution)/shard_map/psum | solution.py:31
  460.8 8.4 %all-reduce.2 = (f32[]{:T(128)}, f32[]{:T(128)}) all-reduce(f32[]{:T(128)} %get-tuple-element.11, f32[]{:T(128)} %get-tuple-element.12), channel_id=1, replica_groups=mesh['gx_0'=8,'gx_1'=2,'gy'=4,'gz'=4] {'gz'}, use_global_device_ids=true, to_apply=%region_4.5 | all-reduce | flops 2 | bytes 16 | tf_op jit(solution)/shard_map/psum | solution.py:31
  482.6 4.1 collective-permute-start.27
  497.4 6.2 %collective-permute-start.31 = (f32[2,1,18]{1,2,0:T(8,128)S(1)}, f32[2,1,18]{1,2,0:T(8,128)S(1)}, u32[]{:S(2)}, u32[]{:S(2)}) collective-permute-start(f32[2,1,18]{1,2,0:T(8,128)S(1)} %get-tuple-element.110), channel_id=1, source_target_pairs={{1,0},{2,1},{3,2},{4,3},{5,4},{6,5},{7,6},{8,7},{9,8},{10,9},{11,1... | collective-permute-start | bytes 440 | tf_op jit(solution)/shard_map/ppermute | solution.py:24
  505.6 5.8 collective-permute-done.30
  583.0 4.2 collective-permute-start.46
  596.3 4.8 fusion.50
  (273 shorter events, 253.8 us)
Async XLA Ops:
  31.4 6.2 %collective-permute-start = (f32[2,512,2]{1,2,0:T(2,128)S(1)}, f32[2,512,2]{1,2,0:T(2,128)S(1)}, u32[]{:S(2)}, u32[]{:S(2)}) collective-permute-start(f32[2,512,2]{1,2,0:T(2,128)S(1)} %get-tuple-element.33), channel_id=1, source_target_pairs={{0,16},{16,32},{32,48},{48,64},{64,80},{80,96},{96,112},{112,128},... | collective-permute-start | bytes 24584 | tf_op jit(solution)/shard_map/ppermute | solution.py:21
  39.6 47.1 %collective-permute-start.3 = (f32[2,2,516]{2,1,0:T(2,128)S(1)}, f32[2,2,516]{2,1,0:T(2,128)S(1)}, u32[]{:S(2)}, u32[]{:S(2)}) collective-permute-start(f32[2,2,516]{2,1,0:T(2,128)S(1)} %copy.134), channel_id=1, source_target_pairs={{1,0},{2,1},{3,2},{4,3},{5,4},{6,5},{7,6},{8,7},{9,8},{10,9},{11,1... | collective-permute-start | bytes 24776 | tf_op jit(solution)/shard_map/ppermute | solution.py:24
  44.7 42.2 %collective-permute-start.2 = (f32[2,2,516]{2,1,0:T(2,128)S(1)}, f32[2,2,516]{2,1,0:T(2,128)S(1)}, u32[]{:S(2)}, u32[]{:S(2)}) collective-permute-start(f32[2,2,516]{2,1,0:T(2,128)S(1)} %copy.133), channel_id=1, source_target_pairs={{0,1},{1,2},{2,3},{3,4},{4,5},{5,6},{6,7},{7,8},{8,9},{9,10},{10,1... | collective-permute-start | bytes 24776 | tf_op jit(solution)/shard_map/ppermute | solution.py:21
  267.0 6.1 collective-permute-start.4
  274.1 18.4 %collective-permute-start.7 = (f32[2,2,260]{1,2,0:T(8,128)}, f32[2,2,260]{1,2,0:T(8,128)S(1)}, u32[]{:S(2)}, u32[]{:S(2)}) collective-permute-start(f32[2,2,260]{1,2,0:T(8,128)} %get-tuple-element.57), channel_id=1, source_target_pairs={{1,0},{2,1},{3,2},{4,3},{5,4},{6,5},{7,6},{8,7},{9,8},{10,9},{11,1... | collective-permute-start | bytes 12488 | tf_op jit(solution)/shard_map/ppermute | solution.py:24
  280.1 13.1 %collective-permute-start.6 = (f32[2,2,260]{1,2,0:T(8,128)}, f32[2,2,260]{1,2,0:T(8,128)}, u32[]{:S(2)}, u32[]{:S(2)}) collective-permute-start(f32[2,2,260]{1,2,0:T(8,128)} %get-tuple-element.56), channel_id=1, source_target_pairs={{0,1},{1,2},{2,3},{3,4},{4,5},{5,6},{6,7},{7,8},{8,9},{9,10},{10,1... | collective-permute-start | bytes 12488 | tf_op jit(solution)/shard_map/ppermute | solution.py:21
  339.9 6.1 collective-permute-start.8
  346.8 10.5 %collective-permute-start.11 = (f32[2,2,132]{1,2,0:T(8,128)}, f32[2,2,132]{1,2,0:T(8,128)S(1)}, u32[]{:S(2)}, u32[]{:S(2)}) collective-permute-start(f32[2,2,132]{1,2,0:T(8,128)} %get-tuple-element.74), channel_id=1, source_target_pairs={{1,0},{2,1},{3,2},{4,3},{5,4},{6,5},{7,6},{8,7},{9,8},{10,9},{11,1... | collective-permute-start | bytes 6344 | tf_op jit(solution)/shard_map/ppermute | solution.py:24
  352.8 9.1 %collective-permute-start.10 = (f32[2,2,132]{1,2,0:T(8,128)S(1)}, f32[2,2,132]{1,2,0:T(8,128)S(1)}, u32[]{:S(2)}, u32[]{:S(2)}) collective-permute-start(f32[2,2,132]{1,2,0:T(8,128)S(1)} %get-tuple-element.73), channel_id=1, source_target_pairs={{0,1},{1,2},{2,3},{3,4},{4,5},{5,6},{6,7},{7,8},{8,9},{9,10},{10,1... | collective-permute-start | bytes 6344 | tf_op jit(solution)/shard_map/ppermute | solution.py:21
  381.9 6.8 %collective-permute-start.15 = (f32[2,2,68]{1,2,0:T(8,128)S(1)}, f32[2,2,68]{1,2,0:T(8,128)S(1)}, u32[]{:S(2)}, u32[]{:S(2)}) collective-permute-start(f32[2,2,68]{1,2,0:T(8,128)S(1)} %get-tuple-element.86), channel_id=1, source_target_pairs={{1,0},{2,1},{3,2},{4,3},{5,4},{6,5},{7,6},{8,7},{9,8},{10,9},{11,1... | collective-permute-start | bytes 3272 | tf_op jit(solution)/shard_map/ppermute | solution.py:24
  383.8 8.4 %collective-permute-start.14 = (f32[2,2,68]{1,2,0:T(8,128)S(1)}, f32[2,2,68]{1,2,0:T(8,128)S(1)}, u32[]{:S(2)}, u32[]{:S(2)}) collective-permute-start(f32[2,2,68]{1,2,0:T(8,128)S(1)} %get-tuple-element.85), channel_id=1, source_target_pairs={{0,1},{1,2},{2,3},{3,4},{4,5},{5,6},{6,7},{7,8},{8,9},{9,10},{10,1... | collective-permute-start | bytes 3272 | tf_op jit(solution)/shard_map/ppermute | solution.py:21
  405.2 8.0 %collective-permute-start.18 = (f32[2,2,36]{1,2,0:T(8,128)S(1)}, f32[2,2,36]{1,2,0:T(8,128)S(1)}, u32[]{:S(2)}, u32[]{:S(2)}) collective-permute-start(f32[2,2,36]{1,2,0:T(8,128)S(1)} %get-tuple-element.97), channel_id=1, source_target_pairs={{0,1},{1,2},{2,3},{3,4},{4,5},{5,6},{6,7},{7,8},{8,9},{9,10},{10,1... | collective-permute-start | bytes 1736 | tf_op jit(solution)/shard_map/ppermute | solution.py:21
  422.5 6.6 %collective-permute-start.23 = (f32[2,2,20]{1,2,0:T(8,128)S(1)}, f32[2,2,20]{1,2,0:T(8,128)S(1)}, u32[]{:S(2)}, u32[]{:S(2)}) collective-permute-start(f32[2,2,20]{1,2,0:T(8,128)S(1)} %get-tuple-element.112), channel_id=1, source_target_pairs={{1,0},{2,1},{3,2},{4,3},{5,4},{6,5},{7,6},{8,7},{9,8},{10,9},{11,1... | collective-permute-start | bytes 968 | tf_op jit(solution)/shard_map/ppermute | solution.py:24
  424.4 7.8 %collective-permute-start.22 = (f32[2,2,20]{1,2,0:T(8,128)S(1)}, f32[2,2,20]{1,2,0:T(8,128)S(1)}, u32[]{:S(2)}, u32[]{:S(2)}) collective-permute-start(f32[2,2,20]{1,2,0:T(8,128)S(1)} %get-tuple-element.111), channel_id=1, source_target_pairs={{0,1},{1,2},{2,3},{3,4},{4,5},{5,6},{6,7},{7,8},{8,9},{9,10},{10,1... | collective-permute-start | bytes 968 | tf_op jit(solution)/shard_map/ppermute | solution.py:21
  478.6 8.0 %collective-permute-start.26 = (f32[2,1,10]{1,2,0:T(8,128)S(1)}, f32[2,1,10]{1,2,0:T(8,128)S(1)}, u32[]{:S(2)}, u32[]{:S(2)}) collective-permute-start(f32[2,1,10]{1,2,0:T(8,128)S(1)} %get-tuple-element.117), channel_id=1, source_target_pairs={{0,1},{1,2},{2,3},{3,4},{4,5},{5,6},{6,7},{7,8},{8,9},{9,10},{10,1... | collective-permute-start | bytes 248 | tf_op jit(solution)/shard_map/ppermute | solution.py:21
  497.4 8.1 %collective-permute-start.31 = (f32[2,1,18]{1,2,0:T(8,128)S(1)}, f32[2,1,18]{1,2,0:T(8,128)S(1)}, u32[]{:S(2)}, u32[]{:S(2)}) collective-permute-start(f32[2,1,18]{1,2,0:T(8,128)S(1)} %get-tuple-element.110), channel_id=1, source_target_pairs={{1,0},{2,1},{3,2},{4,3},{5,4},{6,5},{7,6},{8,7},{9,8},{10,9},{11,1... | collective-permute-start | bytes 440 | tf_op jit(solution)/shard_map/ppermute | solution.py:24
  503.5 7.8 %collective-permute-start.30 = (f32[2,1,18]{1,2,0:T(8,128)S(1)}, f32[2,1,18]{1,2,0:T(8,128)S(1)}, u32[]{:S(2)}, u32[]{:S(2)}) collective-permute-start(f32[2,1,18]{1,2,0:T(8,128)S(1)} %get-tuple-element.109), channel_id=1, source_target_pairs={{0,1},{1,2},{2,3},{3,4},{4,5},{5,6},{6,7},{7,8},{8,9},{9,10},{10,1... | collective-permute-start | bytes 440 | tf_op jit(solution)/shard_map/ppermute | solution.py:21
  522.5 8.0 %collective-permute-start.34 = (f32[2,1,34]{1,2,0:T(8,128)S(1)}, f32[2,1,34]{1,2,0:T(8,128)S(1)}, u32[]{:S(2)}, u32[]{:S(2)}) collective-permute-start(f32[2,1,34]{1,2,0:T(8,128)S(1)} %get-tuple-element.95), channel_id=1, source_target_pairs={{0,1},{1,2},{2,3},{3,4},{4,5},{5,6},{6,7},{7,8},{8,9},{9,10},{10,1... | collective-permute-start | bytes 824 | tf_op jit(solution)/shard_map/ppermute | solution.py:21
  539.9 6.2 %collective-permute-start.39 = (f32[2,1,66]{1,2,0:T(8,128)S(1)}, f32[2,1,66]{1,2,0:T(8,128)S(1)}, u32[]{:S(2)}, u32[]{:S(2)}) collective-permute-start(f32[2,1,66]{1,2,0:T(8,128)S(1)} %get-tuple-element.84), channel_id=1, source_target_pairs={{1,0},{2,1},{3,2},{4,3},{5,4},{6,5},{7,6},{8,7},{9,8},{10,9},{11,1... | collective-permute-start | bytes 1592 | tf_op jit(solution)/shard_map/ppermute | solution.py:24
  541.8 8.4 %collective-permute-start.38 = (f32[2,1,66]{1,2,0:T(8,128)S(1)}, f32[2,1,66]{1,2,0:T(8,128)S(1)}, u32[]{:S(2)}, u32[]{:S(2)}) collective-permute-start(f32[2,1,66]{1,2,0:T(8,128)S(1)} %get-tuple-element.83), channel_id=1, source_target_pairs={{0,1},{1,2},{2,3},{3,4},{4,5},{5,6},{6,7},{7,8},{8,9},{9,10},{10,1... | collective-permute-start | bytes 1592 | tf_op jit(solution)/shard_map/ppermute | solution.py:21
  559.6 6.9 %collective-permute-start.43 = (f32[2,1,130]{1,2,0:T(8,128)S(1)}, f32[2,1,130]{1,2,0:T(8,128)S(1)}, u32[]{:S(2)}, u32[]{:S(2)}) collective-permute-start(f32[2,1,130]{1,2,0:T(8,128)S(1)} %get-tuple-element.72), channel_id=1, source_target_pairs={{1,0},{2,1},{3,2},{4,3},{5,4},{6,5},{7,6},{8,7},{9,8},{10,9},{11,1... | collective-permute-start | bytes 3128 | tf_op jit(solution)/shard_map/ppermute | solution.py:24
  561.5 9.1 %collective-permute-start.42 = (f32[2,1,130]{1,2,0:T(8,128)S(1)}, f32[2,1,130]{1,2,0:T(8,128)S(1)}, u32[]{:S(2)}, u32[]{:S(2)}) collective-permute-start(f32[2,1,130]{1,2,0:T(8,128)S(1)} %get-tuple-element.71), channel_id=1, source_target_pairs={{0,1},{1,2},{2,3},{3,4},{4,5},{5,6},{6,7},{7,8},{8,9},{9,10},{10,1... | collective-permute-start | bytes 3128 | tf_op jit(solution)/shard_map/ppermute | solution.py:21
  581.1 8.4 %collective-permute-start.47 = (f32[2,1,258]{1,2,0:T(8,128)S(1)}, f32[2,1,258]{1,2,0:T(8,128)S(1)}, u32[]{:S(2)}, u32[]{:S(2)}) collective-permute-start(f32[2,1,258]{1,2,0:T(8,128)S(1)} %get-tuple-element.55), channel_id=1, source_target_pairs={{1,0},{2,1},{3,2},{4,3},{5,4},{6,5},{7,6},{8,7},{9,8},{10,9},{11,1... | collective-permute-start | bytes 6200 | tf_op jit(solution)/shard_map/ppermute | solution.py:24
  583.0 10.5 %collective-permute-start.46 = (f32[2,1,258]{1,2,0:T(8,128)S(1)}, f32[2,1,258]{1,2,0:T(8,128)S(1)}, u32[]{:S(2)}, u32[]{:S(2)}) collective-permute-start(f32[2,1,258]{1,2,0:T(8,128)S(1)} %get-tuple-element.54), channel_id=1, source_target_pairs={{0,1},{1,2},{2,3},{3,4},{4,5},{5,6},{6,7},{7,8},{8,9},{9,10},{10,1... | collective-permute-start | bytes 6200 | tf_op jit(solution)/shard_map/ppermute | solution.py:21
  (30 other events, 168.0 us)
where the time goes:
time: 620 us; the launch traced here: 614 us
  local copies, waits for them, and re-layouts  307 us (50%)
  starting transfers between devices  133 us (21%)
  waiting for transfers between devices  86 us (14%)
  other arithmetic  49.7 us (8%)
  blocking collectives  35.6 us (6%)
    slice x24, local copies, waits for them, and re-layouts, reduce_padded(): rows = rows + KERN[tap] * padded[..., tap:tap + rows_out:2, :]  214 us
    ppermute x24, waiting for transfers between devices, extended(): lax.ppermute(lax.slice_in_dim(block, block.shape[dim] - width, None, axis...  80.7 us
    ppermute x24, starting transfers between devices, extended(): lax.ppermute(lax.slice_in_dim(block, block.shape[dim] - width, None, axis...  68.9 us
    ppermute x24, starting transfers between devices, extended(): lax.ppermute(lax.slice_in_dim(block, 0, width, axis=dim), axis, backward)  63.6 us
    slice x6, local copies, waits for them, and re-layouts, reduce_padded(): rows = KERN[0] * padded[..., 0:rows_out:2, :]  53.7 us
    psum x4, blocking collectives, over_axes(): x = lax.psum(x, axis)  35.6 us
    mul x1, other arithmetic, local(): pair = jnp.stack([weight * (heights + offset), weight])  23.3 us
  transfers between devices with their start and end apart: 48, of which 25 were waited for; matrix products, arithmetic and copies ran while one was open for 9% of the time, Pallas kernels for 0%

commit v1 on v0

v1 whole, which is shorter than its diff:
```python
import jax
import jax.numpy as jnp
import numpy as np
from jax import lax
from jax.experimental import pallas as pl
from jax.experimental.pallas import tpu as pltpu
from jax.sharding import PartitionSpec as P

SCENES = 16
LEVELS = 6
TILE = 512
KERN = (0.0625, 0.25, 0.375, 0.25, 0.0625)
ROWS = ("gy", "gz")
COLS = "gx"

N = [TILE >> level for level in range(LEVELS + 1)]
R = [0, 272, 144, 80, 48, 32, 32]
A = [560, 304, 176, 112, 80, 80, 40]
W = [512, 384, 256, 128, 128, 128, 128]
STRIP = [0, 0, 384, 640, 768, 896, 1024]
STRIPS = 1152
BLOCK = [0, 0, 272, 416, 496, 544, 576]
BLOCKS = 608
HIGH = [0, 256, 128, 0, 0, 0, 0]
TURN = [0, 0, 0, 64, 96, 112, 120]
VMEM = 40 * 1024 * 1024


def reduce_matrix(rows, cols, shift):
    out = np.zeros((rows, cols), np.float32)
    for s in range(cols):
        for tap in range(5):
            t = 2 * s - 2 - shift + tap
            if 0 <= t < rows:
                out[t, s] = KERN[tap]
    return out.astype(jnp.bfloat16)


def expand_matrix(rows, cols, shift):
    out = np.zeros((rows, cols), np.float32)
    for c in range(cols):
        s = c + shift
        j = s // 2
        taps = ((j, 0.5), (j + 1, 0.5)) if s % 2 == 0 else ((j, 0.125), (j + 1, 0.75), (j + 2, 0.125))
        for t, value in taps:
            if 0 <= t < rows:
                out[t, c] = value
    return out.astype(jnp.bfloat16)


def times(x, matrix):
    hi = x.astype(jnp.bfloat16)
    rest = x - hi.astype(jnp.float32)
    mid = rest.astype(jnp.bfloat16)
    lo = (rest - mid.astype(jnp.float32)).astype(jnp.bfloat16)
    out = jnp.dot(hi, matrix, preferred_element_type=jnp.float32)
    out = out + jnp.dot(mid, matrix, preferred_element_type=jnp.float32)
    return out + jnp.dot(lo, matrix, preferred_element_type=jnp.float32)


def load(ref, arr, at):
    return jnp.concatenate([ref[arr, tile, at, :] for tile in range(ref.shape[1])], axis=1)


def store(ref, arr, at, value):
    for tile in range(value.shape[1] // 128):
        ref[arr, tile, at, :] = value[:, 128 * tile : 128 * tile + 128]


def row_place():
    return lax.axis_index("gy") * lax.axis_size("gz") + lax.axis_index("gz")


def in_grid(shape, n, rows, cols):
    def side(dim, place, count):
        s = lax.broadcasted_iota(jnp.int32, shape, dim)
        low = jnp.where(place == 0, 1, 0)
        high = jnp.where(place == count - 1, n, n + 2)
        return (s >= low) & (s <= high)

    return side(0, row_place(), rows) & side(1, lax.axis_index(COLS), cols)


def halves(num, den):
    lane = lax.broadcasted_iota(jnp.int32, num.shape, 1)
    return jnp.where(lane < 64, num, den)


def roll(x, shift, axis):
    return pltpu.roll(x, shift % x.shape[axis], axis) if shift % x.shape[axis] else x


def pyramid(rows, cols, offset, weight, heights, ids, first, later, shifted, *refs):
    levels, (low_cols, high_cols, message, base) = refs[:LEVELS], refs[LEVELS:]
    step = 32
    for arr in range(2):
        store(base, arr, slice(0, 8), jnp.zeros((8, TILE), jnp.float32))
        store(base, arr, slice(8 + TILE, A[0]), jnp.zeros((A[0] - 8 - TILE, TILE), jnp.float32))

    def cells(i, _):
        at = pl.ds(pl.multiple_of(i * step, step), step)
        to = pl.ds(pl.multiple_of(i * step + 8, 8), step)
        which = ids[at, :]
        bits = [(which & (1 << b)) != 0 for b in range(4)]

        def lookup(table):
            values = [table[s] for s in range(SCENES)]
            for b in range(4):
                values = [
                    jnp.where(bits[b], values[2 * k + 1], values[2 * k]) for k in range(len(values) // 2)
                ]
            return values[0]

        w = lookup(weight)
        h = heights[at, :] + lookup(offset)
        shifted[at, :] = h
        store(base, 0, to, w * h)
        store(base, 1, to, w)
        return 0

    lax.fori_loop(0, TILE // step, cells, 0)

    for level in range(1, LEVELS + 1):
        source = base if level == 1 else levels[level - 2]
        target = levels[level - 1]
        start = 4 if level == 1 else 5
        size = R[level]
        matrix = first[...] if level == 1 else later[: W[level - 1], : W[level]]
        mask = in_grid((size, W[level]), N[level], rows, cols)
        for arr in range(2):
            taps = [load(source, arr, pl.ds(start + k, size, stride=2)) for k in range(5)]
            tall = KERN[0] * (taps[0] + taps[4]) + KERN[1] * (taps[1] + taps[3]) + KERN[2] * taps[2]
            part = jnp.where(mask, times(tall, matrix), 0.0)
            store(target, arr, slice(0, 8), jnp.zeros((8, W[level]), jnp.float32))
            store(target, arr, slice(8, 8 + size), part)
            if A[level] > 8 + size:
                rest = A[level] - 8 - size
                store(target, arr, slice(8 + size, A[level]), jnp.zeros((rest, W[level]), jnp.float32))

    row = row_place()
    sub = lax.broadcasted_iota(jnp.int32, (8, 128), 0)
    message[...] = jnp.zeros(message.shape, jnp.float32)
    totals = [jnp.sum(levels[LEVELS - 1][arr, 0, 8 : 8 + R[LEVELS], :]) for arr in range(2)]
    plain = jnp.where(sub == 3, totals[0], jnp.where(sub == 7, totals[1], 0.0))

    def strips(level, at):
        ref = levels[level - 1]
        num = load(ref, 0, slice(at, at + 8))
        den = pltpu.roll(load(ref, 1, slice(at, at + 8)), 4, 0)
        sub = lax.broadcasted_iota(jnp.int32, num.shape, 0)
        return jnp.where(sub < 3, num, jnp.where((sub > 3) & (sub < 7), den, 0.0))

    top = STRIP[LEVELS]
    for slot in range(rows):
        message[slot, :, top : top + 128] = plain

    @pl.when(row > 0)
    def _():
        for level in range(1, LEVELS + 1):
            packed = strips(level, 8)
            if level == LEVELS:
                packed = packed + plain
            message[row - 1, :, STRIP[level] : STRIP[level] + W[level]] = packed

    @pl.when(row < rows - 1)
    def _():
        for level in range(1, LEVELS + 1):
            packed = strips(level, 8 + N[level])
            if level == LEVELS:
                packed = packed + plain
            message[row + 1, :, STRIP[level] : STRIP[level] + W[level]] = packed

    for level in range(1, LEVELS + 1):
        size, high, turn = R[level], HIGH[level] // 128, TURN[level]
        ref = levels[level - 1]
        to = slice(BLOCK[level], BLOCK[level] + size)
        low_cols[to, :] = halves(ref[0, 0, 8 : 8 + size, :], roll(ref[1, 0, 8 : 8 + size, :], 64, 1))
        high_cols[to, :] = halves(
            roll(ref[0, high, 8 : 8 + size, :], turn, 1),
            roll(ref[1, high, 8 : 8 + size, :], turn + 64, 1),
        )


def from_rows(rows, message, level):
    row = row_place()
    out = []
    for place in (row - 1, row + 1):
        there = (place >= 0) & (place < rows)
        got = message[jnp.clip(place, 0, rows - 1), :, STRIP[level] : STRIP[level] + W[level]]
        sub = lax.broadcasted_iota(jnp.int32, got.shape, 0)
        keep = (sub < 3) & there
        out.append((jnp.where(keep, got, 0.0), jnp.where(keep, pltpu.roll(got, 4, 0), 0.0)))
    return out


def edges(rows, cols, low_in, high_in, message, low_out, high_out, totals):
    low_out[...] = low_in[...]
    high_out[...] = high_in[...]
    for level in range(1, LEVELS + 1):
        high, turn = HIGH[level], TURN[level]
        for at, (num, den) in zip((0, N[level]), from_rows(rows, message, level)):
            to = slice(BLOCK[level] + at, BLOCK[level] + at + 8)
            low_out[to, :] += halves(num[:, 0:128], roll(den[:, 0:128], 64, 1))
            high_out[to, :] += halves(
                roll(num[:, high : high + 128], turn, 1), roll(den[:, high : high + 128], turn + 64, 1)
            )
    top = STRIP[LEVELS]
    total = message[0, :, top : top + 128]
    for slot in range(1, rows):
        total = total + message[slot, :, top : top + 128]
    both = halves(total[3:4, :], total[7:8, :])
    for slot in range(cols):
        totals[slot, :, :] = both


def collapse(rows, cols, gain, l1, l2, l3, l4, l5, l6, message, below, above, totals, wider, last, shifted, out, tall, wide, full):
    levels = (l1, l2, l3, l4, l5, l6)
    total = totals[0, :, :]
    for slot in range(1, cols):
        total = total + totals[slot, :, :]
    mean = total[0:1, 0:1] / total[0:1, 64:65]

    def ratio(level):
        size, n, high = R[level], N[level], HIGH[level] // 128
        ref = levels[level - 1]
        strips = from_rows(rows, message, level)
        lane = lax.broadcasted_iota(jnp.int32, (size, 128), 1)
        at = slice(BLOCK[level], BLOCK[level] + size)
        for arr in range(2):
            store(full, arr, slice(0, size), load(ref, arr, slice(8, 8 + size)))
            for first, pair in zip((0, n), strips):
                for tile in range(W[level] // 128):
                    full[arr, tile, first : first + 8, :] += pair[arr][:, 128 * tile : 128 * tile + 128]
            low = jnp.where(lane < 3, roll(below[at, :], 64 * arr, 1), 0.0)
            up = jnp.where(lane < 3, roll(above[at, :], 64 * arr, 1), 0.0)
            full[arr, 0, 0:size, :] += low
            full[arr, high, 0:size, :] += roll(up, n, 1)
        mask = in_grid((size, W[level]), n, rows, cols)
        num, den = (load(full, arr, slice(0, size))[:, : W[level]] for arr in range(2))
        return mask, jnp.where(mask, num / jnp.where(mask, den, 1.0), 0.0)

    mask, value = ratio(LEVELS)
    piece = jnp.where(mask, mean - gain[LEVELS - 1] * value, 0.0)
    for level in range(LEVELS - 1, 0, -1):
        size, half = R[level], R[level] // 2
        tall[0 : R[level + 1], 0 : W[level]] = times(piece, wider[: W[level + 1], : W[level]])
        a, b, c = (tall[k : k + half, 0 : W[level]] for k in range(3))
        mask, value = ratio(level)
        even, odd = 0.5 * (a + b), 0.125 * (a + c) + 0.75 * b
        for tile in range(W[level] // 128):
            lanes = slice(128 * tile, 128 * tile + 128)
            wide[tile, pl.ds(0, half, stride=2), :] = even[:, lanes]
            wide[tile, pl.ds(1, half, stride=2), :] = odd[:, lanes]
        grown = jnp.concatenate([wide[tile, 0:size, :] for tile in range(W[level] // 128)], axis=1)
        change = gain[level] - gain[level - 1]
        piece = jnp.where(mask, change * value + grown, 0.0)
    tall[...] = times(piece, last[...])
    half = TILE // 2
    for tile in range(W[0] // 128):
        lanes = slice(128 * tile, 128 * tile + 128)
        a, b, c = (tall[k : k + half, lanes] for k in range(3))
        wide[tile, pl.ds(0, half, stride=2), :] = 0.125 * (a + c) + 0.75 * b
        wide[tile, pl.ds(1, half, stride=2), :] = 0.5 * (b + c)
        out[:, lanes] = gain[0] * shifted[:, lanes] + wide[tile, :, :]


def solution(mesh):
    rows, cols = mesh.shape["gy"] * mesh.shape["gz"], mesh.shape["gx"]
    first = reduce_matrix(W[0], W[1], 2)
    later = reduce_matrix(W[1], W[2], 1)
    wider = expand_matrix(W[2], W[1], 0)
    last = expand_matrix(W[1], W[0], 1)
    f32 = jnp.float32
    smem, vmem = pl.BlockSpec(memory_space=pltpu.SMEM), pl.BlockSpec(memory_space=pltpu.VMEM)
    params = pltpu.CompilerParams(vmem_limit_bytes=VMEM)
    stored = [jax.ShapeDtypeStruct((2, W[level] // 128, A[level], 128), f32) for level in range(1, LEVELS + 1)]
    block = jax.ShapeDtypeStruct((BLOCKS, 128), f32)

    def local(heights, ids, offset, weight, gain):
        shifted, *rest = pl.pallas_call(
            lambda *refs: pyramid(rows, cols, *refs),
            out_shape=[jax.ShapeDtypeStruct((TILE, TILE), f32), *stored, block, block]
            + [jax.ShapeDtypeStruct((rows, 8, STRIPS), f32)],
            in_specs=[smem, smem] + [vmem] * 4,
            out_specs=[vmem] * 10,
            scratch_shapes=[pltpu.VMEM((2, W[0] // 128, A[0], 128), f32)],
            compiler_params=params,
            name="pyramid",
        )(offset, weight, heights, ids, first, later)
        levels, (low, high, message) = rest[:LEVELS], rest[LEVELS:]
        message = lax.all_to_all(message, ROWS, 0, 0)
        low, high, totals = pl.pallas_call(
            lambda *refs: edges(rows, cols, *refs),
            out_shape=[block, block, jax.ShapeDtypeStruct((cols, 1, 128), f32)],
            in_specs=[vmem] * 3,
            out_specs=[vmem] * 3,
            compiler_params=params,
            name="edges",
        )(low, high, message)
        above = lax.ppermute(low, COLS, [(i + 1, i) for i in range(cols - 1)])
        below = lax.ppermute(high, COLS, [(i, i + 1) for i in range(cols - 1)])
        totals = lax.all_to_all(totals, COLS, 0, 0)
        return pl.pallas_call(
            lambda *refs: collapse(rows, cols, *refs),
            out_shape=jax.ShapeDtypeStruct((TILE, TILE), f32),
            in_specs=[smem] + [vmem] * 13,
            out_specs=vmem,
            scratch_shapes=[pltpu.VMEM((R[1], TILE), f32), pltpu.VMEM((W[0] // 128, TILE, 128), f32)]
            + [pltpu.VMEM((2, W[1] // 128, R[1], 128), f32)],
            compiler_params=params,
            name="collapse",
        )(gain, *levels, message, below, above, totals, wider, last, shifted)

    spec = P(ROWS, COLS)
    return jax.shard_map(
        local, mesh=mesh, in_specs=(spec, spec, P(), P(), P()), out_specs=spec, check_vma=False
    )
```

time: 620 us -> 58.5 us (0.09)
  the two profiles are of different devices: /device:TPU:130 before, /device:TPU:1 now
where the time goes in v1:
time: 58.5 us; the launch traced here: 58.1 us
  blocking collectives  35.1 us (60%)
  Pallas kernels  8.95 us (15%)
  starting transfers between devices  7.69 us (13%)
  local copies, waits for them, and re-layouts  6.32 us (11%)
    all_to_all x1, blocking collectives, local(): message = lax.all_to_all(message, ROWS, 0, 0)  18.4 us
    all_to_all x1, blocking collectives, local(): totals = lax.all_to_all(totals, COLS, 0, 0)  16.7 us
    unnamed x18, local copies, waits for them, and re-layouts  6.32 us
    ppermute x1, starting transfers between devices, local(): below = lax.ppermute(high, COLS, [(i, i + 1) for i in range(cols - 1)])  5.77 us
    pallas_call x1, Pallas kernels, local(): pl.pallas_call(lambda *refs: pyramid(rows, cols, *refs), out_shape=[jax.S...  5.03 us
    pallas_call x1, Pallas kernels, local(): pl.pallas_call(lambda *refs: collapse(rows, cols, *refs), out_shape=jax.S...  3.8 us
    ppermute x1, starting transfers between devices, local(): above = lax.ppermute(low, COLS, [(i + 1, i) for i in range(cols - 1)])  1.92 us
  transfers between devices with their start and end apart: 2, of which 0 were waited for; matrix products, arithmetic and copies ran while one was open for 0% of the time, Pallas kernels for 0%

profile of v1, /device:TPU:1, one launch (start us, length us, event | category | flops | bytes accessed | tf_op | source)
XLA Modules:
  0.0 58.1 jit_solution(14570556322433048610)
XLA Ops:
  0.0 0.0 copy-start
  0.0 1.2 %copy-done = f32[512,512]{1,0:T(8,128)S(1)} copy-done((f32[512,512]{1,0:T(8,128)S(1)}, f32[512,512]{1,0:T(8,128)}, u32[]{:S(2)}) %copy-start) | copy-done | bytes 1048600
  1.2 0.0 copy-start.1
  1.2 1.2 %copy-done.1 = s32[512,512]{1,0:T(8,128)S(1)} copy-done((s32[512,512]{1,0:T(8,128)S(1)}, s32[512,512]{1,0:T(8,128)}, u32[]{:S(2)}) %copy-start.1) | copy-done | bytes 1048600
  2.5 0.0 copy-start.3
  2.5 1.0 %copy-done.3 = bf16[512,384]{1,0:T(8,128)(2,1)S(1)} copy-done((bf16[512,384]{1,0:T(8,128)(2,1)S(1)}, bf16[512,384]{1,0:T(8,128)(2,1)}, u32[]{:S(2)}) %copy-start.3) | copy-done | bytes 393240
  3.4 0.0 copy-start.5
  3.4 0.9 %copy-done.5 = bf16[384,256]{1,0:T(8,128)(2,1)S(1)} copy-done((bf16[384,256]{1,0:T(8,128)(2,1)S(1)}, bf16[384,256]{1,0:T(8,128)(2,1)}, u32[]{:S(2)}) %copy-start.5) | copy-done | bytes 196632
  4.4 0.0 copy-start.6
  4.4 0.7 %copy-done.6 = f32[16]{0:T(128)S(1)} copy-done((f32[16]{0:T(128)S(1)}, f32[16]{0:T(128)}, u32[]{:S(2)}) %copy-start.6) | copy-done | bytes 88
  5.0 0.0 copy-start.7
  5.0 0.7 %copy-done.7 = f32[16]{0:T(128)S(1)} copy-done((f32[16]{0:T(128)S(1)}, f32[16]{0:T(128)}, u32[]{:S(2)}) %copy-start.7) | copy-done | bytes 88
  5.7 5.0 %pyramid.1 = (f32[512,512]{1,0:T(8,128)S(1)}, f32[2,3,304,128]{3,2,1,0:T(8,128)S(1)}, f32[2,2,176,128]{3,2,1,0:T(8,128)S(1)}, f32[2,1,112,128]{3,2,1,0:T(8,128)S...) custom-call(f32[16]{0:T(128)S(1)} %copy-done.6, ...), custom_call_target="tpu_custom_call" | custom-call | tf_op jit(solution)/shard_map/pyramid/pallas_call | solution.py:280
  10.7 18.4 %all_to_all.10.refs_2_.refs_7_ = f32[16,8,1152]{2,1,0:T(8,128)S(1)} all-to-all(f32[16,8,1152]{2,1,0:T(8,128)S(1)} %get-tuple-element.24), channel_id=1, replica_groups=mesh['gx'=16,'gy'=4,'gz'=4] {'gy','gz'}, dimensions={0} | all-to-all | bytes 1179648 | tf_op jit(solution)/shard_map/all_to_all | solution.py:291
  29.1 0.1 edges.1
  29.2 5.8 %collective-permute-start = (f32[608,128]{1,0:T(8,128)S(1)}, f32[608,128]{1,0:T(8,128)S(1)}, u32[]{:S(2)}, u32[]{:S(2)}) collective-permute-start(f32[608,128]{1,0:T(8,128)S(1)} %get-tuple-element.27), channel_id=1, source_target_pairs={{0,16},{16,32},{32,48},{48,64},{64,80},{80,96},{96,112},{112,128},... | collective-permute-start | bytes 933896 | tf_op jit(solution)/shard_map/ppermute | solution.py:301
  35.0 1.9 %collective-permute-start.1 = (f32[608,128]{1,0:T(8,128)S(1)}, f32[608,128]{1,0:T(8,128)S(1)}, u32[]{:S(2)}, u32[]{:S(2)}) collective-permute-start(f32[608,128]{1,0:T(8,128)S(1)} %get-tuple-element.28), channel_id=1, source_target_pairs={{16,0},{32,16},{48,32},{64,48},{80,64},{96,80},{112,96},{128,112},... | collective-permute-start | bytes 933896 | tf_op jit(solution)/shard_map/ppermute | solution.py:300
  36.9 16.7 %all_to_all.11.refs_10_ = f32[16,1,128]{2,1,0:T(1,128)S(1)} all-to-all(f32[16,1,128]{2,1,0:T(1,128)S(1)} %get-tuple-element.29), channel_id=1, replica_groups=mesh['gx'=16,'gy'=4,'gz'=4] {'gx'}, dimensions={0} | all-to-all | bytes 16384 | tf_op jit(solution)/shard_map/all_to_all | solution.py:302
  53.6 0.0 collective-permute-done.refs_8_
  53.6 0.0 collective-permute-done.1.refs_9_
  53.6 0.0 copy-done.2
  53.7 0.0 copy-done.4
  53.7 0.6 %copy-done.8 = f32[6]{0:T(128)S(1)} copy-done((f32[6]{0:T(128)S(1)}, f32[6]{0:T(128)}, u32[]{:S(2)}) %copy-start.8) | copy-done | bytes 48
  54.3 3.8 %collapse.1 = f32[512,512]{1,0:T(8,128)} custom-call(f32[6]{0:T(128)S(1)} %copy-done.8, f32[2,3,304,128]{3,2,1,0:T(8,128)S(1)} %get-tuple-element.18.refs_1_, f32[2,2,176,128]{3,2,1,0:T(8,128)S(1)} %get-tuple-element.19.refs_2_, f32[2,1,112,128]{3,2,1,0:T(8,128)S(1)} %get-tuple-element.20.refs_3_, f32[2,1,80,128]{3,2,1,0:T(8,128)S(1)} %get-tuple-element.21.refs_4_, ...), custom_call_target="tpu_custom_call" | custom-call | tf_op jit(solution)/shard_map/collapse/pallas_call | solution.py:303
  (3 shorter events, 0.0 us)
Async XLA Ops:
  0.0 1.2 %copy-start = (f32[512,512]{1,0:T(8,128)S(1)}, f32[512,512]{1,0:T(8,128)}, u32[]{:S(2)}) copy-start(f32[512,512]{1,0:T(8,128)} %refs_2_.1) | copy-start | bytes 3145732
  1.2 1.2 %copy-start.1 = (s32[512,512]{1,0:T(8,128)S(1)}, s32[512,512]{1,0:T(8,128)}, u32[]{:S(2)}) copy-start(s32[512,512]{1,0:T(8,128)} %refs_3_.1) | copy-start | bytes 3145732
  2.5 1.0 %copy-start.3 = (bf16[512,384]{1,0:T(8,128)(2,1)S(1)}, bf16[512,384]{1,0:T(8,128)(2,1)}, u32[]{:S(2)}) copy-start(bf16[512,384]{1,0:T(8,128)(2,1)} %constant.8.clone.refs_4_) | copy-start | bytes 1179652
  3.4 0.9 %copy-start.5 = (bf16[384,256]{1,0:T(8,128)(2,1)S(1)}, bf16[384,256]{1,0:T(8,128)(2,1)}, u32[]{:S(2)}) copy-start(bf16[384,256]{1,0:T(8,128)(2,1)} %constant.9.clone.refs_5_) | copy-start | bytes 589828
  4.4 0.7 %copy-start.6 = (f32[16]{0:T(128)S(1)}, f32[16]{0:T(128)}, u32[]{:S(2)}) copy-start(f32[16]{0:T(128)} %refs_0_.2) | copy-start | bytes 196
  5.0 0.7 %copy-start.7 = (f32[16]{0:T(128)S(1)}, f32[16]{0:T(128)}, u32[]{:S(2)}) copy-start(f32[16]{0:T(128)} %refs_1_.1) | copy-start | bytes 196
  29.1 24.6 %copy-start.2 = (bf16[384,512]{1,0:T(8,128)(2,1)S(1)}, bf16[384,512]{1,0:T(8,128)(2,1)}, u32[]{:S(2)}) copy-start(bf16[384,512]{1,0:T(8,128)(2,1)} %constant.11.clone.refs_12_) | copy-start | bytes 1179652
  29.1 24.6 %copy-start.4 = (bf16[256,384]{1,0:T(8,128)(2,1)S(1)}, bf16[256,384]{1,0:T(8,128)(2,1)}, u32[]{:S(2)}) copy-start(bf16[256,384]{1,0:T(8,128)(2,1)} %constant.10.clone.refs_11_) | copy-start | bytes 589828
  29.2 24.4 %collective-permute-start = (f32[608,128]{1,0:T(8,128)S(1)}, f32[608,128]{1,0:T(8,128)S(1)}, u32[]{:S(2)}, u32[]{:S(2)}) collective-permute-start(f32[608,128]{1,0:T(8,128)S(1)} %get-tuple-element.27), channel_id=1, source_target_pairs={{0,16},{16,32},{32,48},{48,64},{64,80},{80,96},{96,112},{112,128},... | collective-permute-start | bytes 933896 | tf_op jit(solution)/shard_map/ppermute | solution.py:301
  35.0 18.6 %collective-permute-start.1 = (f32[608,128]{1,0:T(8,128)S(1)}, f32[608,128]{1,0:T(8,128)S(1)}, u32[]{:S(2)}, u32[]{:S(2)}) collective-permute-start(f32[608,128]{1,0:T(8,128)S(1)} %get-tuple-element.28), channel_id=1, source_target_pairs={{16,0},{32,16},{48,32},{64,48},{80,64},{96,80},{112,96},{128,112},... | collective-permute-start | bytes 933896 | tf_op jit(solution)/shard_map/ppermute | solution.py:300
  53.6 0.7 %copy-start.8 = (f32[6]{0:T(128)S(1)}, f32[6]{0:T(128)}, u32[]{:S(2)}) copy-start(f32[6]{0:T(128)} %refs_0_.3) | copy-start | bytes 76

commit v2 on v1

v2 whole, which is shorter than its diff:
```python
import jax
import jax.numpy as jnp
import numpy as np
from jax import lax
from jax.experimental import pallas as pl
from jax.experimental.pallas import tpu as pltpu
from jax.sharding import PartitionSpec as P

SCENES = 16
LEVELS = 6
TILE = 512
KERN = (0.0625, 0.25, 0.375, 0.25, 0.0625)
ROWS = ("gy", "gz")
COLS = "gx"

N = [TILE >> level for level in range(LEVELS + 1)]
R = [0, 272, 144, 80, 48, 32, 32]
A = [560, 304, 176, 112, 80, 80, 40]
W = [512, 384, 256, 128, 128, 128, 128]
STRIP = [0, 0, 384, 640, 768, 896, 1024]
STRIPS = 1280
SLOT = 80
PIECES = [
    (1, 0, 80, 0, 0),
    (1, 80, 80, 1, 0),
    (1, 160, 80, 2, 0),
    (1, 240, 32, 3, 0),
    (6, 0, 32, 3, 32),
    (2, 0, 80, 4, 0),
    (2, 80, 64, 5, 0),
    (3, 0, 80, 6, 0),
    (4, 0, 48, 7, 0),
    (5, 0, 32, 7, 48),
]
ENDS = 336
HIGH = [0, 256, 128, 0, 0, 0, 0]
TURN = [0, 0, 0, 64, 96, 112, 120]
PARTS = 4
VMEM = 40 * 1024 * 1024
FIRST_VMEM = 203 * 256 * 1024


def reduce_matrix(rows, cols, shift):
    t = lax.broadcasted_iota(jnp.int32, (rows, cols), 0)
    s = lax.broadcasted_iota(jnp.int32, (rows, cols), 1)
    d = jnp.abs(t - 2 * s + shift)
    out = jnp.where(d == 2, KERN[0], 0.0)
    return jnp.where(d == 1, KERN[1], jnp.where(d == 0, KERN[2], out)).astype(jnp.bfloat16)


def expand_matrix(rows, cols, shift):
    out = np.zeros((rows, cols), np.float32)
    for c in range(cols):
        s = c + shift
        j = s // 2
        taps = ((j, 0.5), (j + 1, 0.5)) if s % 2 == 0 else ((j, 0.125), (j + 1, 0.75), (j + 2, 0.125))
        for t, value in taps:
            if 0 <= t < rows:
                out[t, c] = value
    return out.astype(jnp.bfloat16)


def with_ends(matrix):
    for k, x in enumerate((*end_vectors(), np.ones(TILE, np.float32))):
        for part in range(3):
            matrix[ENDS + 3 * k + part] = x.astype(jnp.bfloat16)
            x = x - x.astype(jnp.bfloat16).astype(np.float32)
    return matrix


def times(x, matrix):
    hi = x.astype(jnp.bfloat16)
    rest = x - hi.astype(jnp.float32)
    mid = rest.astype(jnp.bfloat16)
    lo = (rest - mid.astype(jnp.float32)).astype(jnp.bfloat16)
    out = jnp.dot(hi, matrix, preferred_element_type=jnp.float32)
    out = out + jnp.dot(mid, matrix, preferred_element_type=jnp.float32)
    return out + jnp.dot(lo, matrix, preferred_element_type=jnp.float32)


def load(ref, arr, at):
    return jnp.concatenate([ref[arr, tile, at, :] for tile in range(ref.shape[1])], axis=1)


def store(ref, arr, at, value):
    for tile in range(value.shape[1] // 128):
        ref[arr, tile, at, :] = value[:, 128 * tile : 128 * tile + 128]


def row_place():
    return lax.axis_index("gy") * lax.axis_size("gz") + lax.axis_index("gz")


def in_grid(shape, n, rows, cols):
    def side(dim, place, count):
        s = lax.broadcasted_iota(jnp.int32, shape, dim)
        low = jnp.where(place == 0, 1, 0)
        high = jnp.where(place == count - 1, n, n + 2)
        return (s >= low) & (s <= high)

    return side(0, row_place(), rows) & side(1, lax.axis_index(COLS), cols)


def roll(x, shift, axis):
    return pltpu.roll(x, shift % x.shape[axis], axis) if shift % x.shape[axis] else x


def three(num, den, low_slot):
    lane = lax.broadcasted_iota(jnp.int32, num.shape, 1)
    at = 8 * low_slot
    num = jnp.where((lane >= at) & (lane < at + 3), roll(num, at, 1), 0.0)
    return jnp.where((lane >= at + 64) & (lane < at + 67), roll(den, at + 64, 1), num)


def pyramid(rows, cols, heights_in, ids_in, tables, shifted, *refs):
    levels, refs = refs[:LEVELS], refs[LEVELS:]
    low_cols, high_cols, even_rows, odd_rows, totals, gains, base = refs[:7]
    heights, ids, first, later, table, sems = refs[7:]
    step, part = 32, TILE // PARTS
    pairs = [(tables, table)]
    for k in range(PARTS):
        at = slice(k * part, k * part + part)
        pairs.append((heights_in.at[at], heights.at[at]))
        pairs.append((ids_in.at[at], ids.at[at]))
    copies = [pltpu.make_async_copy(a, b, sems.at[k]) for k, (a, b) in enumerate(pairs)]
    for copy in copies:
        copy.start()
    first[...] = reduce_matrix(W[0], W[1], 2)
    later[...] = reduce_matrix(W[1], W[2], 1)
    for arr in range(2):
        store(base, arr, slice(0, 8), jnp.zeros((8, TILE), jnp.float32))
        store(base, arr, slice(8 + TILE, A[0]), jnp.zeros((A[0] - 8 - TILE, TILE), jnp.float32))

    def cells(i, _):
        at = pl.ds(pl.multiple_of(i * step, step), step)
        to = pl.ds(pl.multiple_of(i * step + 8, 8), step)
        which = ids[at, :]
        bits = [(which & (1 << b)) != 0 for b in range(4)]

        def lookup(which_table):
            values = [table[which_table, s] for s in range(SCENES)]
            for b in range(4):
                values = [
                    jnp.where(bits[b], values[2 * k + 1], values[2 * k]) for k in range(len(values) // 2)
                ]
            return values[0]

        w = lookup(1)
        h = heights[at, :] + lookup(0)
        shifted[at, :] = h
        store(base, 0, to, w * h)
        store(base, 1, to, w)
        return 0

    copies[0].wait()
    for k in range(PARTS):
        copies[1 + 2 * k].wait()
        copies[2 + 2 * k].wait()
        lax.fori_loop(k * part // step, (k + 1) * part // step, cells, 0)

    for level in range(1, LEVELS + 1):
        source = base if level == 1 else levels[level - 2]
        target = levels[level - 1]
        start = 4 if level == 1 else 5
        size = R[level]
        matrix = first[...] if level == 1 else later[: W[level - 1], : W[level]]
        mask = in_grid((size, W[level]), N[level], rows, cols)
        for arr in range(2):
            taps = [load(source, arr, pl.ds(start + k, size, stride=2)) for k in range(5)]
            tall = KERN[0] * (taps[0] + taps[4]) + KERN[1] * (taps[1] + taps[3]) + KERN[2] * taps[2]
            part = jnp.where(mask, times(tall, matrix), 0.0)
            store(target, arr, slice(0, 8), jnp.zeros((8, W[level]), jnp.float32))
            store(target, arr, slice(8, 8 + size), part)
            if A[level] > 8 + size:
                rest = A[level] - 8 - size
                store(target, arr, slice(8 + size, A[level]), jnp.zeros((rest, W[level]), jnp.float32))

    even = row_place() % 2 == 0
    lane = lax.broadcasted_iota(jnp.int32, (8, 128), 1)
    sub = lax.broadcasted_iota(jnp.int32, (8, 128), 0)
    sums = [jnp.sum(levels[LEVELS - 1][arr, 0, 8 : 8 + R[LEVELS], :]) for arr in range(2)]
    both = jnp.where(lane < 64, sums[0], sums[1])
    totals[...] = both
    even_rows[:, STRIPS - 128 :] = both
    odd_rows[:, STRIPS - 128 :] = both
    gains[...] = sum(jnp.where(sub == k, table[2, k], 0.0) for k in range(LEVELS))

    def strips(level, at):
        ref = levels[level - 1]
        num = load(ref, 0, slice(at, at + 8))
        den = pltpu.roll(load(ref, 1, slice(at, at + 8)), 4, 0)
        sub = lax.broadcasted_iota(jnp.int32, num.shape, 0)
        return jnp.where(sub < 3, num, jnp.where((sub > 3) & (sub < 7), den, 0.0))

    for level in range(1, LEVELS + 1):
        low, high = strips(level, 8), strips(level, 8 + N[level])
        to = slice(STRIP[level], STRIP[level] + W[level])
        even_rows[:, to] = jnp.where(even, high, low)
        odd_rows[:, to] = jnp.where(even, low, high)

    low_cols[...] = jnp.zeros(low_cols.shape, jnp.float32)
    high_cols[...] = jnp.zeros(high_cols.shape, jnp.float32)
    for level, row, size, slot, place in PIECES:
        tile, turn = HIGH[level] // 128, TURN[level]
        num, den = levels[level - 1].at[0], levels[level - 1].at[1]
        at, to = slice(8 + row, 8 + row + size), slice(place, place + size)
        low_cols[to, :] += three(num[0, at, :], den[0, at, :], slot)
        high_cols[to, :] += three(roll(num[tile, at, :], turn, 1), roll(den[tile, at, :], turn, 1), slot)


def from_rows(rows, even_rows, odd_rows, level):
    even = row_place() % 2 == 0
    to = slice(STRIP[level], STRIP[level] + W[level])
    one, two = even_rows[:, to], odd_rows[:, to]
    near = lax.broadcasted_iota(jnp.int32, one.shape, 0) < 3
    out = []
    row = row_place()
    above = (jnp.where(even, two, one), row > 0)
    below = (jnp.where(even, one, two), row < rows - 1)
    for got, there in (above, below):
        keep = near & there
        out.append((jnp.where(keep, got, 0.0), jnp.where(keep, pltpu.roll(got, 4, 0), 0.0)))
    return out


def edges(rows, low_in, high_in, even_rows, odd_rows, totals, even_cols, odd_cols, low, high):
    low[...] = low_in[...]
    high[...] = high_in[...]
    for level in range(1, LEVELS + 1):
        tile, turn = HIGH[level], TURN[level]
        for at, (num, den) in zip((0, N[level]), from_rows(rows, even_rows, odd_rows, level)):
            for which, row, size, slot, place in PIECES:
                if which == level and row <= at < row + size:
                    to = slice(place + at - row, place + at - row + 8)
                    low[to, :] += three(num[:, 0:128], den[:, 0:128], slot)
                    num, den = (roll(x[:, tile : tile + 128], turn, 1) for x in (num, den))
                    high[to, :] += three(num, den, slot)
    even = lax.axis_index(COLS) % 2 == 0
    one, two = low[...], high[...]
    even_cols[0:SLOT, :] = jnp.where(even, two, one)
    odd_cols[0:SLOT, :] = jnp.where(even, one, two)
    even_cols[SLOT:, :] = totals[...]
    odd_cols[SLOT:, :] = totals[...]


def collapse(rows, cols, gains, l1, l2, l3, l4, l5, l6, even_rows, odd_rows, even_cols, odd_cols, wider, last, shifted, out, field, tall, wide, full):
    levels = (l1, l2, l3, l4, l5, l6)
    first_of_pair = lax.axis_index(COLS) % 2 == 0
    gain = [gains[k : k + 1, 0:1] for k in range(LEVELS)]

    def ratio(level):
        size, n, high = R[level], N[level], HIGH[level] // 128
        ref = levels[level - 1]
        strips = from_rows(rows, even_rows, odd_rows, level)
        for arr in range(2):
            store(full, arr, slice(0, size), load(ref, arr, slice(8, 8 + size)))
            for first, pair in zip((0, n), strips):
                for tile in range(W[level] // 128):
                    full[arr, tile, first : first + 8, :] += pair[arr][:, 128 * tile : 128 * tile + 128]
        for which, row, count, slot, place in PIECES:
            if which != level:
                continue
            one, two = even_cols[place : place + count, :], odd_cols[place : place + count, :]
            below = jnp.where(first_of_pair, two, one)
            above = jnp.where(first_of_pair, one, two)
            lane = lax.broadcasted_iota(jnp.int32, one.shape, 1)
            for arr in range(2):
                at = 8 * slot + 64 * arr
                low = jnp.where(lane < 3, roll(below, -at, 1), 0.0)
                up = n % 128
                up = jnp.where((lane >= up) & (lane < up + 3), roll(above, n - at, 1), 0.0)
                full[arr, 0, row : row + count, :] += low
                full[arr, high, row : row + count, :] += up
        mask = in_grid((size, W[level]), n, rows, cols)
        num, den = (load(full, arr, slice(0, size))[:, : W[level]] for arr in range(2))
        return mask, jnp.where(mask, num / jnp.where(mask, den, 1.0), 0.0)

    mask, value = ratio(LEVELS)
    piece = jnp.where(mask, -gain[LEVELS - 1] * value, 0.0)
    for level in range(LEVELS - 1, 0, -1):
        size, half = R[level], R[level] // 2
        tall[0 : R[level + 1], 0 : W[level]] = times(piece, wider[: W[level + 1], : W[level]])
        a, b, c = (tall[k : k + half, 0 : W[level]] for k in range(3))
        mask, value = ratio(level)
        even, odd = 0.5 * (a + b), 0.125 * (a + c) + 0.75 * b
        for tile in range(W[level] // 128):
            lanes = slice(128 * tile, 128 * tile + 128)
            wide[tile, pl.ds(0, half, stride=2), :] = even[:, lanes]
            wide[tile, pl.ds(1, half, stride=2), :] = odd[:, lanes]
        grown = jnp.concatenate([wide[tile, 0:size, :] for tile in range(W[level] // 128)], axis=1)
        change = gain[level] - gain[level - 1]
        piece = jnp.where(mask, change * value + grown, 0.0)
    tall[...] = times(piece, last[...])
    half = TILE // 2
    for tile in range(W[0] // 128):
        lanes = slice(128 * tile, 128 * tile + 128)
        a, b, c = (tall[k : k + half, lanes] for k in range(3))
        wide[tile, pl.ds(0, half, stride=2), :] = 0.125 * (a + c) + 0.75 * b
        wide[tile, pl.ds(1, half, stride=2), :] = 0.5 * (b + c)
        out[:, lanes] = gain[0] * shifted[:, lanes] + wide[tile, :, :]
    ones_expanded(rows, cols, last, field)


def end_vectors():
    low, high = np.ones(4 * N[LEVELS]), np.ones(4 * N[LEVELS])
    for _ in range(LEVELS):
        wide = [np.concatenate([[0.0], x, [1.0]]) for x in (low,)] + [np.concatenate([[1.0], high, [0.0]])]
        done = []
        for x in wide:
            a, b, c = x[:-2], x[1:-1], x[2:]
            done.append(np.stack([(a + 6 * b + c) / 8, (b + c) / 2], axis=1).reshape(-1))
        low, high = done
    return np.stack([low[:TILE], high[-TILE:]]).astype(np.float32)


def ones_expanded(rows, cols, last, field):
    ends = last[ENDS : ENDS + 16, :]

    def pick(place, count, order):
        kind = jnp.where(place == 0, 0, jnp.where(place == count - 1, 1, 2))
        k = lax.broadcasted_iota(jnp.int32, (16, 16), 0)
        source = lax.broadcasted_iota(jnp.int32, (16, 16), 1)
        hit = jnp.zeros((16, 16), jnp.bool_)
        for at, which in enumerate(order):
            hit = hit | ((k == at) & (source == 3 * kind + which))
        chosen = jnp.where(hit, 1.0, 0.0).astype(jnp.bfloat16)
        return jnp.dot(chosen, ends, preferred_element_type=jnp.float32).astype(jnp.bfloat16)

    a = pick(row_place(), rows, (0, 0, 1, 1, 0, 2))
    b = pick(lax.axis_index(COLS), cols, (0, 1, 0, 1, 2, 0))
    field[...] = lax.dot_general(a, b, (((0,), (0,)), ((), ())), preferred_element_type=jnp.float32)


def finish(rest, field, totals, out, done, sems):
    mean = totals[0:1, 0:1] / totals[0:1, 64:65]
    part = TILE // PARTS
    copies = []
    for k in range(PARTS):
        at = slice(k * part, k * part + part)
        done[at, :] = rest[at, :] + mean * field[at, :]
        copies.append(pltpu.make_async_copy(done.at[at], out.at[at], sems.at[k]))
        copies[-1].start()
    for copy in copies:
        copy.wait()


def swaps(count, first):
    return [p for i in range(first, count - 1, 2) for p in ((i, i + 1), (i + 1, i))]


def solution(mesh):
    rows, cols = mesh.shape["gy"] * mesh.shape["gz"], mesh.shape["gx"]
    wider = expand_matrix(W[2], W[1], 0)
    last = with_ends(expand_matrix(W[1], W[0], 1))
    f32 = jnp.float32
    anyw, vmem = pl.BlockSpec(memory_space=pltpu.HBM), pl.BlockSpec(memory_space=pltpu.VMEM)
    params = pltpu.CompilerParams(vmem_limit_bytes=VMEM)
    stored = [jax.ShapeDtypeStruct((2, W[level] // 128, A[level], 128), f32) for level in range(1, LEVELS + 1)]
    block = jax.ShapeDtypeStruct((SLOT, 128), f32)
    strip = jax.ShapeDtypeStruct((8, STRIPS), f32)
    small = jax.ShapeDtypeStruct((8, 128), f32)
    tile = jax.ShapeDtypeStruct((TILE, TILE), f32)

    def ring(axis, size, unit=1):
        def at(i, j):
            return [(i * unit + u, j * unit + u) for u in range(unit)]

        def both(pairs):
            return [p for i, j in pairs for p in at(i, j) + at(j, i)]

        rounds = []
        if size > 1:
            rounds.append(both([(i, i + 1) for i in range(0, size, 2)]))
        if size == 4:
            rounds.append(both([(0, 3), (1, 2)]))
        if size == 8:
            rounds.append(both([(0, 2), (1, 3), (4, 6), (5, 7)]))
            rounds.append(both([(i, 7 - i) for i in range(4)]))
        return [(axis, r) for r in rounds]

    def add(totals, rounds):
        for axis, pairs in rounds:
            totals = totals + lax.ppermute(totals, axis, pairs)
        return totals

    gy, gz, gx = ring("gy", mesh.shape["gy"]), ring("gz", mesh.shape["gz"]), ring(COLS, cols // 2, 2)

    def local(heights, ids, offset, weight, gain):
        def row(x):
            return jnp.pad(x, (0, 128 - x.shape[0]))[None]

        tables = jnp.concatenate([row(offset), row(weight), row(gain), jnp.zeros((5, 128), f32)], axis=0)
        shifted, *rest = pl.pallas_call(
            lambda *refs: pyramid(rows, cols, *refs),
            out_shape=[tile, *stored, block, block, strip, strip, small, small],
            in_specs=[anyw] * 3,
            out_specs=[vmem] * 13,
            scratch_shapes=[
                pltpu.VMEM((2, W[0] // 128, A[0], 128), f32),
                pltpu.VMEM((TILE, TILE), f32),
                pltpu.VMEM((TILE, TILE), jnp.int32),
                pltpu.VMEM((W[0], W[1]), jnp.bfloat16),
                pltpu.VMEM((W[1], W[2]), jnp.bfloat16),
                pltpu.SMEM((8, 128), f32),
                pltpu.SemaphoreType.DMA((1 + 2 * PARTS,)),
            ],
            compiler_params=pltpu.CompilerParams(vmem_limit_bytes=FIRST_VMEM),
            name="pyramid",
        )(heights, ids, tables)
        levels, (low, high, even_rows, odd_rows, totals, gains) = rest[:LEVELS], rest[LEVELS:]
        even_rows = lax.ppermute(even_rows, ROWS, swaps(rows, 0))
        odd_rows = lax.ppermute(odd_rows, ROWS, swaps(rows, 1) + [(0, rows - 1), (rows - 1, 0)])
        totals = add(totals + even_rows[:, STRIPS - 128 :], gz[1:])
        even_cols, odd_cols = pl.pallas_call(
            lambda *refs: edges(rows, *refs),
            out_shape=[jax.ShapeDtypeStruct((SLOT + 8, 128), f32)] * 2,
            in_specs=[vmem] * 5,
            out_specs=[vmem] * 2,
            scratch_shapes=[pltpu.VMEM((SLOT, 128), f32)] * 2,
            compiler_params=params,
            name="edges",
        )(low, high, even_rows, odd_rows, totals)
        even_cols = lax.ppermute(even_cols, COLS, swaps(cols, 0))
        odd_cols = lax.ppermute(odd_cols, COLS, swaps(cols, 1))
        totals = add(totals + even_cols[SLOT:], gx[:2] + gy + gx[2:])
        rest, field = pl.pallas_call(
            lambda *refs: collapse(rows, cols, *refs),
            out_shape=[tile, tile],
            in_specs=[vmem] * 14,
            out_specs=[vmem] * 2,
            scratch_shapes=[pltpu.VMEM((R[1], TILE), f32), pltpu.VMEM((W[0] // 128, TILE, 128), f32)]
            + [pltpu.VMEM((2, W[1] // 128, R[1], 128), f32)],
            compiler_params=params,
            name="collapse",
        )(gains, *levels, even_rows, odd_rows, even_cols, odd_cols, wider, last, shifted)
        return pl.pallas_call(
            finish,
            out_shape=tile,
            in_specs=[vmem] * 3,
            out_specs=pl.BlockSpec(memory_space=pl.ANY),
            scratch_shapes=[pltpu.VMEM((TILE, TILE), f32), pltpu.SemaphoreType.DMA((PARTS,))],
            compiler_params=params,
            name="finish",
        )(rest, field, totals)

    spec = P(ROWS, COLS)
    return jax.shard_map(
        local, mesh=mesh, in_specs=(spec, spec, P(), P(), P()), out_specs=spec, check_vma=False
    )
```

time: 58.5 us -> 47.4 us (0.81)
  the two profiles are of different devices: /device:TPU:1 before, /device:TPU:32 now
where the time goes in v2:
time: 47.4 us; the launch traced here: 47.2 us
  starting transfers between devices  19.9 us (42%)
  waiting for transfers between devices  16.5 us (35%)
  Pallas kernels  9.25 us (20%)
  local copies, waits for them, and re-layouts  1.34 us (3%)
    ppermute x6, waiting for transfers between devices, add(): totals = totals + lax.ppermute(totals, axis, pairs)  16.5 us
    ppermute x6, starting transfers between devices, add(): totals = totals + lax.ppermute(totals, axis, pairs)  11.7 us
    pallas_call x1, Pallas kernels, local(): pl.pallas_call(lambda *refs: pyramid(rows, cols, *refs), out_shape=[tile,...  5.37 us
    ppermute x1, starting transfers between devices, local(): lax.ppermute(odd_rows, ROWS, swaps(rows, 1) + [(0, rows - 1), (rows - 1,...  4.38 us
    pallas_call x1, Pallas kernels, local(): pl.pallas_call(lambda *refs: collapse(rows, cols, *refs), out_shape=[tile...  2.56 us
    ppermute x1, starting transfers between devices, local(): odd_cols = lax.ppermute(odd_cols, COLS, swaps(cols, 1))  2.11 us
    ppermute x1, starting transfers between devices, local(): even_rows = lax.ppermute(even_rows, ROWS, swaps(rows, 0))  1.66 us
    pallas_call x1, Pallas kernels, local(): pl.pallas_call(finish, out_shape=tile, in_specs=[vmem] * 3, out_specs=pl....  1.14 us
  transfers between devices with their start and end apart: 10, of which 5 were waited for; matrix products, arithmetic and copies ran while one was open for 0% of the time, Pallas kernels for 5%

profile of v2, /device:TPU:32, one launch (start us, length us, event | category | flops | bytes accessed | tf_op | source)
XLA Modules:
  0.0 47.2 jit_solution(3725618545304460390)
XLA Ops:
  0.0 0.7 %pad_bitcast_fusion.2 = f32[1,128]{1,0:T(1,128)S(1)} fusion(f32[16]{0:T(128)} %param.9), kind=kLoop, calls=%fused_computation.5 | loop fusion | bytes 576 | tf_op jit(solution)/shard_map/broadcast_in_dim | solution.py:390
  0.7 0.1 pad.17.clone
  0.7 0.6 %copy-done.2 = f32[6]{0:T(128)S(1)} copy-done((f32[6]{0:T(128)S(1)}, f32[6]{0:T(128)}, u32[]{:S(2)}) %copy-start.2) | copy-done | bytes 48
  1.3 0.0 copy-done.3
  1.3 0.1 maximum_maximum_fusion.refs_2_
  1.4 5.4 %pyramid.1 = (f32[512,512]{1,0:T(8,128)S(1)}, f32[2,3,304,128]{3,2,1,0:T(8,128)S(1)}, f32[2,2,176,128]{3,2,1,0:T(8,128)S(1)}, f32[2,1,112,128]{3,2,1,0:T(8,128)S...) custom-call(f32[512,512]{1,0:T(8,128)} %refs_0_.1, ...), custom_call_target="tpu_custom_call" | custom-call | tf_op jit(solution)/shard_map/pyramid/pallas_call | solution.py:393
  6.8 0.0 copy-start.1
  6.8 1.7 %collective-permute-start = (f32[8,1280]{1,0:T(8,128)S(1)}, f32[8,1280]{1,0:T(8,128)S(1)}, u32[]{:S(2)}, u32[]{:S(2)}) collective-permute-start(f32[8,1280]{1,0:T(8,128)S(1)} %get-tuple-element.29), channel_id=1, source_target_pairs={{0,1},{1,0},{2,3},{3,2},{4,5},{5,4},{6,7},{7,6},{8,9},{9,8},{10,11... | collective-permute-start | bytes 122888 | tf_op jit(solution)/shard_map/ppermute | solution.py:411
  8.5 4.4 %collective-permute-start.1 = (f32[8,1280]{1,0:T(8,128)S(1)}, f32[8,1280]{1,0:T(8,128)S(1)}, u32[]{:S(2)}, u32[]{:S(2)}) collective-permute-start(f32[8,1280]{1,0:T(8,128)S(1)} %get-tuple-element.30), channel_id=1, source_target_pairs={{1,2},{2,1},{3,4},{4,3},{5,6},{6,5},{7,8},{8,7},{9,10},{10,9},{11,... | collective-permute-start | bytes 122888 | tf_op jit(solution)/shard_map/ppermute | solution.py:412
  12.8 1.1 %collective-permute-start.2 = (f32[8,128]{1,0:T(8,128)S(1)}, f32[8,128]{1,0:T(8,128)S(1)}, u32[]{:S(2)}, u32[]{:S(2)}) collective-permute-start(f32[8,128]{1,0:T(8,128)S(1)} %slice_add_fusion.1), channel_id=1, source_target_pairs={{0,3},{3,0},{1,2},{2,1},{4,7},{7,4},{5,6},{6,5},{8,11},{11,8},{9,1... | collective-permute-start | bytes 12296 | tf_op jit(solution)/shard_map/ppermute | solution.py:383
  13.9 3.8 %collective-permute-done.2 = f32[8,128]{1,0:T(8,128)S(1)} collective-permute-done((f32[8,128]{1,0:T(8,128)S(1)}, f32[8,128]{1,0:T(8,128)S(1)}, u32[]{:S(2)}, u32[]{:S(2)}) %collective-permute-start.2) | collective-permute-done | bytes 4128 | tf_op jit(solution)/shard_map/ppermute | solution.py:383
  17.7 0.2 edges.1
  17.9 0.1 collective-permute-start.3
  18.0 2.1 %collective-permute-start.4 = (f32[88,128]{1,0:T(8,128)S(1)}, f32[88,128]{1,0:T(8,128)S(1)}, u32[]{:S(2)}, u32[]{:S(2)}) collective-permute-start(f32[88,128]{1,0:T(8,128)S(1)} %get-tuple-element.35), channel_id=1, source_target_pairs={{16,32},{32,16},{48,64},{64,48},{80,96},{96,80},{112,128},{128,112... | collective-permute-start | bytes 135176 | tf_op jit(solution)/shard_map/ppermute | solution.py:424
  20.1 0.1 collective-permute-start.5
  20.2 3.6 %collective-permute-done.5 = f32[8,128]{1,0:T(8,128)S(1)} collective-permute-done((f32[8,128]{1,0:T(8,128)S(1)}, f32[8,128]{1,0:T(8,128)S(1)}, u32[]{:S(2)}, u32[]{:S(2)}) %collective-permute-start.5) | collective-permute-done | bytes 4128 | tf_op jit(solution)/shard_map/ppermute | solution.py:383
  23.8 3.3 %collective-permute-start.6 = (f32[8,128]{1,0:T(8,128)S(1)}, f32[8,128]{1,0:T(8,128)S(1)}, u32[]{:S(2)}, u32[]{:S(2)}) collective-permute-start(f32[8,128]{1,0:T(8,128)S(1)} %add.33), channel_id=1, source_target_pairs={{0,64},{16,80},{64,0},{80,16},{32,96},{48,112},{96,32},{112,48},{1... | collective-permute-start | bytes 12296 | tf_op jit(solution)/shard_map/ppermute | solution.py:383
  27.1 1.6 %collective-permute-done.6 = f32[8,128]{1,0:T(8,128)S(1)} collective-permute-done((f32[8,128]{1,0:T(8,128)S(1)}, f32[8,128]{1,0:T(8,128)S(1)}, u32[]{:S(2)}, u32[]{:S(2)}) %collective-permute-start.6) | collective-permute-done | bytes 4128 | tf_op jit(solution)/shard_map/ppermute | solution.py:383
  28.7 3.6 %collective-permute-done.7 = f32[8,128]{1,0:T(8,128)S(1)} collective-permute-done((f32[8,128]{1,0:T(8,128)S(1)}, f32[8,128]{1,0:T(8,128)S(1)}, u32[]{:S(2)}, u32[]{:S(2)}) %collective-permute-start.7) | collective-permute-done | bytes 4128 | tf_op jit(solution)/shard_map/ppermute | solution.py:383
  32.3 0.8 %collective-permute-start.8 = (f32[8,128]{1,0:T(8,128)S(1)}, f32[8,128]{1,0:T(8,128)S(1)}, u32[]{:S(2)}, u32[]{:S(2)}) collective-permute-start(f32[8,128]{1,0:T(8,128)S(1)} %add.35), channel_id=1, source_target_pairs={{0,12},{12,0},{4,8},{8,4},{1,13},{13,1},{5,9},{9,5},{2,14},{14,2},... | collective-permute-start | bytes 12296 | tf_op jit(solution)/shard_map/ppermute | solution.py:383
  33.1 4.0 %collective-permute-done.8 = f32[8,128]{1,0:T(8,128)S(1)} collective-permute-done((f32[8,128]{1,0:T(8,128)S(1)}, f32[8,128]{1,0:T(8,128)S(1)}, u32[]{:S(2)}, u32[]{:S(2)}) %collective-permute-start.8) | collective-permute-done | bytes 4128 | tf_op jit(solution)/shard_map/ppermute | solution.py:383
  37.1 6.4 %collective-permute-start.9 = (f32[8,128]{1,0:T(8,128)S(1)}, f32[8,128]{1,0:T(8,128)S(1)}, u32[]{:S(2)}, u32[]{:S(2)}) collective-permute-start(f32[8,128]{1,0:T(8,128)S(1)} %add.36), channel_id=1, source_target_pairs={{0,224},{16,240},{224,0},{240,16},{32,192},{48,208},{192,32},{208,... | collective-permute-start | bytes 12296 | tf_op jit(solution)/shard_map/ppermute | solution.py:383
  43.5 2.6 %collapse.1 = (f32[512,512]{1,0:T(8,128)S(1)}, f32[512,512]{1,0:T(8,128)S(1)}) custom-call(f32[8,128]{1,0:T(8,128)S(1)} %get-tuple-element.22.refs_0_, f32[2,3,304,128]{3,2,1,0:T(8,128)S(1)} %get-tuple-element.23.refs_1_, f32[2,2,176,128]{3,2,1,0:T(8,128)S(1)} %get-tuple-element.24.refs_2_, f32[2,1,112,128]{3,2,1,0:T(8,128)S(1)} %get-tuple-element.25.refs_3_, ...), custom_call_target="tpu_custom_call" | custom-call | tf_op jit(solution)/shard_map/collapse/pallas_call | solution.py:426
  46.1 1.1 %finish.1 = f32[512,512]{1,0:T(8,128)} custom-call(f32[512,512]{1,0:T(8,128)S(1)} %get-tuple-element.37.rest, f32[512,512]{1,0:T(8,128)S(1)} %get-tuple-element.38.field, f32[8,128]{1,0:T(8,128)S(1)} %add.37.totals), custom_call_target="tpu_custom_call" | custom-call | tf_op jit(solution)/shard_map/finish/pallas_call | solution.py:436
  (21 shorter events, 0.1 us)
Async XLA Ops:
  0.7 0.7 %copy-start.2 = (f32[6]{0:T(128)S(1)}, f32[6]{0:T(128)}, u32[]{:S(2)}) copy-start(f32[6]{0:T(128)} %param.11) | copy-start | bytes 76
  0.7 0.7 %copy-start.3 = (f32[16]{0:T(128)S(1)}, f32[16]{0:T(128)}, u32[]{:S(2)}) copy-start(f32[16]{0:T(128)} %param.10) | copy-start | bytes 196
  1.4 42.1 %copy-start = (bf16[384,512]{1,0:T(8,128)(2,1)S(1)}, bf16[384,512]{1,0:T(8,128)(2,1)}, u32[]{:S(2)}) copy-start(bf16[384,512]{1,0:T(8,128)(2,1)} %constant.9.clone.refs_12_) | copy-start | bytes 1179652
  6.8 36.7 %copy-start.1 = (bf16[256,384]{1,0:T(8,128)(2,1)S(1)}, bf16[256,384]{1,0:T(8,128)(2,1)}, u32[]{:S(2)}) copy-start(bf16[256,384]{1,0:T(8,128)(2,1)} %constant.8.clone.refs_11_) | copy-start | bytes 589828
  6.8 6.0 %collective-permute-start = (f32[8,1280]{1,0:T(8,128)S(1)}, f32[8,1280]{1,0:T(8,128)S(1)}, u32[]{:S(2)}, u32[]{:S(2)}) collective-permute-start(f32[8,1280]{1,0:T(8,128)S(1)} %get-tuple-element.29), channel_id=1, source_target_pairs={{0,1},{1,0},{2,3},{3,2},{4,5},{5,4},{6,7},{7,6},{8,9},{9,8},{10,11... | collective-permute-start | bytes 122888 | tf_op jit(solution)/shard_map/ppermute | solution.py:411
  8.5 9.2 %collective-permute-start.1 = (f32[8,1280]{1,0:T(8,128)S(1)}, f32[8,1280]{1,0:T(8,128)S(1)}, u32[]{:S(2)}, u32[]{:S(2)}) collective-permute-start(f32[8,1280]{1,0:T(8,128)S(1)} %get-tuple-element.30), channel_id=1, source_target_pairs={{1,2},{2,1},{3,4},{4,3},{5,6},{6,5},{7,8},{8,7},{9,10},{10,9},{11,... | collective-permute-start | bytes 122888 | tf_op jit(solution)/shard_map/ppermute | solution.py:412
  12.8 4.8 %collective-permute-start.2 = (f32[8,128]{1,0:T(8,128)S(1)}, f32[8,128]{1,0:T(8,128)S(1)}, u32[]{:S(2)}, u32[]{:S(2)}) collective-permute-start(f32[8,128]{1,0:T(8,128)S(1)} %slice_add_fusion.1), channel_id=1, source_target_pairs={{0,3},{3,0},{1,2},{2,1},{4,7},{7,4},{5,6},{6,5},{8,11},{11,8},{9,1... | collective-permute-start | bytes 12296 | tf_op jit(solution)/shard_map/ppermute | solution.py:383
  17.9 2.2 %collective-permute-start.3 = (f32[88,128]{1,0:T(8,128)S(1)}, f32[88,128]{1,0:T(8,128)S(1)}, u32[]{:S(2)}, u32[]{:S(2)}) collective-permute-start(f32[88,128]{1,0:T(8,128)S(1)} %get-tuple-element.34), channel_id=1, source_target_pairs={{0,16},{16,0},{32,48},{48,32},{64,80},{80,64},{96,112},{112,96},{1... | collective-permute-start | bytes 135176 | tf_op jit(solution)/shard_map/ppermute | solution.py:423
  18.0 25.5 %collective-permute-start.4 = (f32[88,128]{1,0:T(8,128)S(1)}, f32[88,128]{1,0:T(8,128)S(1)}, u32[]{:S(2)}, u32[]{:S(2)}) collective-permute-start(f32[88,128]{1,0:T(8,128)S(1)} %get-tuple-element.35), channel_id=1, source_target_pairs={{16,32},{32,16},{48,64},{64,48},{80,96},{96,80},{112,128},{128,112... | collective-permute-start | bytes 135176 | tf_op jit(solution)/shard_map/ppermute | solution.py:424
  20.1 3.7 %collective-permute-start.5 = (f32[8,128]{1,0:T(8,128)S(1)}, f32[8,128]{1,0:T(8,128)S(1)}, u32[]{:S(2)}, u32[]{:S(2)}) collective-permute-start(f32[8,128]{1,0:T(8,128)S(1)} %slice_add_fusion), channel_id=1, source_target_pairs={{0,32},{16,48},{32,0},{48,16},{64,96},{80,112},{96,64},{112,80},{1... | collective-permute-start | bytes 12296 | tf_op jit(solution)/shard_map/ppermute | solution.py:383
  23.8 4.9 %collective-permute-start.6 = (f32[8,128]{1,0:T(8,128)S(1)}, f32[8,128]{1,0:T(8,128)S(1)}, u32[]{:S(2)}, u32[]{:S(2)}) collective-permute-start(f32[8,128]{1,0:T(8,128)S(1)} %add.33), channel_id=1, source_target_pairs={{0,64},{16,80},{64,0},{80,16},{32,96},{48,112},{96,32},{112,48},{1... | collective-permute-start | bytes 12296 | tf_op jit(solution)/shard_map/ppermute | solution.py:383
  28.7 3.6 %collective-permute-start.7 = (f32[8,128]{1,0:T(8,128)S(1)}, f32[8,128]{1,0:T(8,128)S(1)}, u32[]{:S(2)}, u32[]{:S(2)}) collective-permute-start(f32[8,128]{1,0:T(8,128)S(1)} %add.34), channel_id=1, source_target_pairs={{0,4},{4,0},{8,12},{12,8},{1,5},{5,1},{9,13},{13,9},{2,6},{6,2},{1... | collective-permute-start | bytes 12296 | tf_op jit(solution)/shard_map/ppermute | solution.py:383
  32.3 4.8 %collective-permute-start.8 = (f32[8,128]{1,0:T(8,128)S(1)}, f32[8,128]{1,0:T(8,128)S(1)}, u32[]{:S(2)}, u32[]{:S(2)}) collective-permute-start(f32[8,128]{1,0:T(8,128)S(1)} %add.35), channel_id=1, source_target_pairs={{0,12},{12,0},{4,8},{8,4},{1,13},{13,1},{5,9},{9,5},{2,14},{14,2},... | collective-permute-start | bytes 12296 | tf_op jit(solution)/shard_map/ppermute | solution.py:383
  37.1 9.0 %collective-permute-start.9 = (f32[8,128]{1,0:T(8,128)S(1)}, f32[8,128]{1,0:T(8,128)S(1)}, u32[]{:S(2)}, u32[]{:S(2)}) collective-permute-start(f32[8,128]{1,0:T(8,128)S(1)} %add.36), channel_id=1, source_target_pairs={{0,224},{16,240},{224,0},{240,16},{32,192},{48,208},{192,32},{208,... | collective-permute-start | bytes 12296 | tf_op jit(solution)/shard_map/ppermute | solution.py:383

commit v3 on v2

--- a/solution.py
+++ b/solution.py
@@ -18,7 +18,7 @@
 A = [560, 304, 176, 112, 80, 80, 40]
 W = [512, 384, 256, 128, 128, 128, 128]
 STRIP = [0, 0, 384, 640, 768, 896, 1024]
-STRIPS = 1280
+STRIPS = 1152
 SLOT = 80
 PIECES = [
     (1, 0, 80, 0, 0),
@@ -32,12 +32,11 @@
     (4, 0, 48, 7, 0),
     (5, 0, 32, 7, 48),
 ]
-ENDS = 336
 HIGH = [0, 256, 128, 0, 0, 0, 0]
 TURN = [0, 0, 0, 64, 96, 112, 120]
 PARTS = 4
 VMEM = 40 * 1024 * 1024
-FIRST_VMEM = 203 * 256 * 1024
+FIRST_VMEM = 50 * 1024 * 1024
 
 
 def reduce_matrix(rows, cols, shift):
@@ -60,14 +59,6 @@
     return out.astype(jnp.bfloat16)
 
 
-def with_ends(matrix):
-    for k, x in enumerate((*end_vectors(), np.ones(TILE, np.float32))):
-        for part in range(3):
-            matrix[ENDS + 3 * k + part] = x.astype(jnp.bfloat16)
-            x = x - x.astype(jnp.bfloat16).astype(np.float32)
-    return matrix
-
-
 def times(x, matrix):
     hi = x.astype(jnp.bfloat16)
     rest = x - hi.astype(jnp.float32)
@@ -112,10 +103,23 @@
     return jnp.where((lane >= at + 64) & (lane < at + 67), roll(den, at + 64, 1), num)
 
 
-def pyramid(rows, cols, heights_in, ids_in, tables, shifted, *refs):
-    levels, refs = refs[:LEVELS], refs[LEVELS:]
-    low_cols, high_cols, even_rows, odd_rows, totals, gains, base = refs[:7]
-    heights, ids, first, later, table, sems = refs[7:]
+def ones_expanded(place, count, tall, wide):
+    for level in range(LEVELS, 0, -1):
+        s = lax.broadcasted_iota(jnp.int32, (R[level], 128), 0)
+        inside = (s >= jnp.where(place == 0, 1, 0)) & (s <= jnp.where(place == count - 1, N[level], N[level] + 2))
+        x = 1.0 if level == LEVELS else wide[0 : R[level], :]
+        tall[0 : R[level], :] = jnp.where(inside, x, 0.0)
+        half = R[level - 1] // 2 if level > 1 else TILE // 2
+        a, b, c = (tall[k : k + half, :] for k in range(3))
+        even, odd = 0.5 * (a + b), 0.125 * (a + c) + 0.75 * b
+        if level == 1:
+            even, odd = odd, 0.5 * (b + c)
+        wide[pl.ds(0, half, stride=2), :] = even
+        wide[pl.ds(1, half, stride=2), :] = odd
+
+
+def scenes(rows, cols, heights_in, ids_in, tables, *refs):
+    base, (shifted, totals, gains, ups, downs, heights, ids, tall, wide, table, sems) = refs[:8], refs[8:]
     step, part = 32, TILE // PARTS
     pairs = [(tables, table)]
     for k in range(PARTS):
@@ -125,48 +129,72 @@
     copies = [pltpu.make_async_copy(a, b, sems.at[k]) for k, (a, b) in enumerate(pairs)]
     for copy in copies:
         copy.start()
-    first[...] = reduce_matrix(W[0], W[1], 2)
-    later[...] = reduce_matrix(W[1], W[2], 1)
-    for arr in range(2):
-        store(base, arr, slice(0, 8), jnp.zeros((8, TILE), jnp.float32))
-        store(base, arr, slice(8 + TILE, A[0]), jnp.zeros((A[0] - 8 - TILE, TILE), jnp.float32))
-
-    def cells(i, _):
+    for ref in base:
+        ref[0:8, :] = jnp.zeros((8, 128), jnp.float32)
+        ref[8 + TILE :, :] = jnp.zeros((A[0] - 8 - TILE, 128), jnp.float32)
+    ones_expanded(lax.axis_index(COLS), cols, tall, wide)
+    for tile in range(4):
+        downs[:, 128 * tile : 128 * tile + 128] = wide[128 * tile : 128 * tile + 128, :].T[0:8, :]
+    ones_expanded(row_place(), rows, tall, wide)
+    ups[...] = wide[...]
+
+    def cells(i, sums):
         at = pl.ds(pl.multiple_of(i * step, step), step)
         to = pl.ds(pl.multiple_of(i * step + 8, 8), step)
         which = ids[at, :]
         bits = [(which & (1 << b)) != 0 for b in range(4)]
 
-        def lookup(which_table):
-            values = [table[which_table, s] for s in range(SCENES)]
+        def lookup(first):
+            values = [table[first + s] for s in range(SCENES)]
             for b in range(4):
                 values = [
                     jnp.where(bits[b], values[2 * k + 1], values[2 * k]) for k in range(len(values) // 2)
                 ]
             return values[0]
 
-        w = lookup(1)
+        w = lookup(SCENES)
         h = heights[at, :] + lookup(0)
         shifted[at, :] = h
-        store(base, 0, to, w * h)
-        store(base, 1, to, w)
-        return 0
+        up = ups[at, :]
+        up = jnp.concatenate([up] * (W[0] // 128), axis=1)
+        out = []
+        for arr, value in enumerate((w * h, w)):
+            for tile in range(W[0] // 128):
+                base[4 * arr + tile][to, :] = value[:, 128 * tile : 128 * tile + 128]
+            value = value * up
+            out.append(sums[arr] + sum(value[8 * k : 8 * k + 8] for k in range(step // 8)))
+        return tuple(out)
 
     copies[0].wait()
+    sums = (jnp.zeros((8, TILE), jnp.float32),) * 2
     for k in range(PARTS):
         copies[1 + 2 * k].wait()
         copies[2 + 2 * k].wait()
-        lax.fori_loop(k * part // step, (k + 1) * part // step, cells, 0)
-
+        sums = lax.fori_loop(k * part // step, (k + 1) * part // step, cells, sums)
+    sums = [jnp.sum(x * downs[...]) for x in sums]
+    lane = lax.broadcasted_iota(jnp.int32, (8, 128), 1)
+    sub = lax.broadcasted_iota(jnp.int32, (8, 128), 0)
+    totals[...] = jnp.where(lane < 64, sums[0], sums[1])
+    gains[...] = sum(jnp.where(sub == k, table[2 * SCENES + k], 0.0) for k in range(LEVELS))
+
+
+def pyramid(rows, cols, *refs):
+    base, refs = refs[:8], refs[8:]
+    levels, (even_rows, odd_rows, first, later) = refs[:LEVELS], refs[LEVELS:]
+    first[...] = reduce_matrix(W[0], W[1], 2)
+    later[...] = reduce_matrix(W[1], W[2], 1)
     for level in range(1, LEVELS + 1):
-        source = base if level == 1 else levels[level - 2]
         target = levels[level - 1]
         start = 4 if level == 1 else 5
         size = R[level]
         matrix = first[...] if level == 1 else later[: W[level - 1], : W[level]]
         mask = in_grid((size, W[level]), N[level], rows, cols)
         for arr in range(2):
-            taps = [load(source, arr, pl.ds(start + k, size, stride=2)) for k in range(5)]
+            places = [pl.ds(start + k, size, stride=2) for k in range(5)]
+            if level == 1:
+                taps = [jnp.concatenate([base[4 * arr + t][at, :] for t in range(4)], axis=1) for at in places]
+            else:
+                taps = [load(levels[level - 2], arr, at) for at in places]
             tall = KERN[0] * (taps[0] + taps[4]) + KERN[1] * (taps[1] + taps[3]) + KERN[2] * taps[2]
             part = jnp.where(mask, times(tall, matrix), 0.0)
             store(target, arr, slice(0, 8), jnp.zeros((8, W[level]), jnp.float32))
@@ -176,15 +204,6 @@
                 store(target, arr, slice(8 + size, A[level]), jnp.zeros((rest, W[level]), jnp.float32))
 
     even = row_place() % 2 == 0
-    lane = lax.broadcasted_iota(jnp.int32, (8, 128), 1)
-    sub = lax.broadcasted_iota(jnp.int32, (8, 128), 0)
-    sums = [jnp.sum(levels[LEVELS - 1][arr, 0, 8 : 8 + R[LEVELS], :]) for arr in range(2)]
-    both = jnp.where(lane < 64, sums[0], sums[1])
-    totals[...] = both
-    even_rows[:, STRIPS - 128 :] = both
-    odd_rows[:, STRIPS - 128 :] = both
-    gains[...] = sum(jnp.where(sub == k, table[2, k], 0.0) for k in range(LEVELS))
-
     def strips(level, at):
         ref = levels[level - 1]
         num = load(ref, 0, slice(at, at + 8))
@@ -198,6 +217,9 @@
         even_rows[:, to] = jnp.where(even, high, low)
         odd_rows[:, to] = jnp.where(even, low, high)
 
+
+def pack(*refs):
+    levels, (low_cols, high_cols) = refs[:LEVELS], refs[LEVELS:]
     low_cols[...] = jnp.zeros(low_cols.shape, jnp.float32)
     high_cols[...] = jnp.zeros(high_cols.shape, jnp.float32)
     for level, row, size, slot, place in PIECES:
@@ -243,7 +265,7 @@
     odd_cols[SLOT:, :] = totals[...]
 
 
-def collapse(rows, cols, gains, l1, l2, l3, l4, l5, l6, even_rows, odd_rows, even_cols, odd_cols, wider, last, shifted, out, field, tall, wide, full):
+def collapse(rows, cols, gains, l1, l2, l3, l4, l5, l6, even_rows, odd_rows, even_cols, odd_cols, wider, last, shifted, out, tall, wide, full):
     levels = (l1, l2, l3, l4, l5, l6)
     first_of_pair = lax.axis_index(COLS) % 2 == 0
     gain = [gains[k : k + 1, 0:1] for k in range(LEVELS)]
@@ -298,46 +320,18 @@
         wide[tile, pl.ds(0, half, stride=2), :] = 0.125 * (a + c) + 0.75 * b
         wide[tile, pl.ds(1, half, stride=2), :] = 0.5 * (b + c)
         out[:, lanes] = gain[0] * shifted[:, lanes] + wide[tile, :, :]
-    ones_expanded(rows, cols, last, field)
-
-
-def end_vectors():
-    low, high = np.ones(4 * N[LEVELS]), np.ones(4 * N[LEVELS])
-    for _ in range(LEVELS):
-        wide = [np.concatenate([[0.0], x, [1.0]]) for x in (low,)] + [np.concatenate([[1.0], high, [0.0]])]
-        done = []
-        for x in wide:
-            a, b, c = x[:-2], x[1:-1], x[2:]
-            done.append(np.stack([(a + 6 * b + c) / 8, (b + c) / 2], axis=1).reshape(-1))
-        low, high = done
-    return np.stack([low[:TILE], high[-TILE:]]).astype(np.float32)
-
-
-def ones_expanded(rows, cols, last, field):
-    ends = last[ENDS : ENDS + 16, :]
-
-    def pick(place, count, order):
-        kind = jnp.where(place == 0, 0, jnp.where(place == count - 1, 1, 2))
-        k = lax.broadcasted_iota(jnp.int32, (16, 16), 0)
-        source = lax.broadcasted_iota(jnp.int32, (16, 16), 1)
-        hit = jnp.zeros((16, 16), jnp.bool_)
-        for at, which in enumerate(order):
-            hit = hit | ((k == at) & (source == 3 * kind + which))
-        chosen = jnp.where(hit, 1.0, 0.0).astype(jnp.bfloat16)
-        return jnp.dot(chosen, ends, preferred_element_type=jnp.float32).astype(jnp.bfloat16)
-
-    a = pick(row_place(), rows, (0, 0, 1, 1, 0, 2))
-    b = pick(lax.axis_index(COLS), cols, (0, 1, 0, 1, 2, 0))
-    field[...] = lax.dot_general(a, b, (((0,), (0,)), ((), ())), preferred_element_type=jnp.float32)
-
-
-def finish(rest, field, totals, out, done, sems):
+
+
+def finish(rest, ups, downs, totals, out, done, sems):
     mean = totals[0:1, 0:1] / totals[0:1, 64:65]
     part = TILE // PARTS
     copies = []
     for k in range(PARTS):
         at = slice(k * part, k * part + part)
-        done[at, :] = rest[at, :] + mean * field[at, :]
+        up = mean * ups[at, :]
+        for tile in range(W[0] // 128):
+            lanes = slice(128 * tile, 128 * tile + 128)
+            done[at, lanes] = rest[at, lanes] + up * downs[0:1, lanes]
         copies.append(pltpu.make_async_copy(done.at[at], out.at[at], sems.at[k]))
         copies[-1].start()
     for copy in copies:
@@ -351,7 +345,7 @@
 def solution(mesh):
     rows, cols = mesh.shape["gy"] * mesh.shape["gz"], mesh.shape["gx"]
     wider = expand_matrix(W[2], W[1], 0)
-    last = with_ends(expand_matrix(W[1], W[0], 1))
+    last = expand_matrix(W[1], W[0], 1)
     f32 = jnp.float32
     anyw, vmem = pl.BlockSpec(memory_space=pltpu.HBM), pl.BlockSpec(memory_space=pltpu.VMEM)
     params = pltpu.CompilerParams(vmem_limit_bytes=VMEM)
@@ -386,31 +380,49 @@
     gy, gz, gx = ring("gy", mesh.shape["gy"]), ring("gz", mesh.shape["gz"]), ring(COLS, cols // 2, 2)
 
     def local(heights, ids, offset, weight, gain):
-        def row(x):
-            return jnp.pad(x, (0, 128 - x.shape[0]))[None]
-
-        tables = jnp.concatenate([row(offset), row(weight), row(gain), jnp.zeros((5, 128), f32)], axis=0)
-        shifted, *rest = pl.pallas_call(
-            lambda *refs: pyramid(rows, cols, *refs),
-            out_shape=[tile, *stored, block, block, strip, strip, small, small],
+        tables = jnp.concatenate([offset, weight, gain])
+        *base, shifted, totals, gains, ups, downs = pl.pallas_call(
+            lambda *refs: scenes(rows, cols, *refs),
+            out_shape=[jax.ShapeDtypeStruct((A[0], 128), f32)] * 8
+            + [tile, small, small, jax.ShapeDtypeStruct((TILE, 128), f32), jax.ShapeDtypeStruct((8, TILE), f32)],
             in_specs=[anyw] * 3,
             out_specs=[vmem] * 13,
             scratch_shapes=[
-                pltpu.VMEM((2, W[0] // 128, A[0], 128), f32),
                 pltpu.VMEM((TILE, TILE), f32),
                 pltpu.VMEM((TILE, TILE), jnp.int32),
-                pltpu.VMEM((W[0], W[1]), jnp.bfloat16),
-                pltpu.VMEM((W[1], W[2]), jnp.bfloat16),
-                pltpu.SMEM((8, 128), f32),
+                pltpu.VMEM((R[1], 128), f32),
+                pltpu.VMEM((TILE, 128), f32),
+                pltpu.SMEM((2 * SCENES + LEVELS,), f32),
                 pltpu.SemaphoreType.DMA((1 + 2 * PARTS,)),
             ],
             compiler_params=pltpu.CompilerParams(vmem_limit_bytes=FIRST_VMEM),
+            name="scenes",
+        )(heights, ids, tables)
+        totals = add(totals, gz[1:])
+        *levels, even_rows, odd_rows = pl.pallas_call(
+            lambda *refs: pyramid(rows, cols, *refs),
+            out_shape=[*stored, strip, strip],
+            in_specs=[vmem] * 8,
+            out_specs=[vmem] * (LEVELS + 2),
+            scratch_shapes=[
+                pltpu.VMEM((W[0], W[1]), jnp.bfloat16),
+                pltpu.VMEM((W[1], W[2]), jnp.bfloat16),
+            ],
+            compiler_params=params,
             name="pyramid",
-        )(heights, ids, tables)
-        levels, (low, high, even_rows, odd_rows, totals, gains) = rest[:LEVELS], rest[LEVELS:]
+        )(*base)
+        low, high = pl.pallas_call(
+            pack,
+            out_shape=[block, block],
+            in_specs=[vmem] * LEVELS,
+            out_specs=[vmem] * 2,
+            compiler_params=params,
+            name="pack",
+        )(*levels)
+        even_rows = jnp.concatenate([even_rows, totals], axis=1)
         even_rows = lax.ppermute(even_rows, ROWS, swaps(rows, 0))
         odd_rows = lax.ppermute(odd_rows, ROWS, swaps(rows, 1) + [(0, rows - 1), (rows - 1, 0)])
-        totals = add(totals + even_rows[:, STRIPS - 128 :], gz[1:])
+        totals = add(totals + even_rows[:, STRIPS:], gy[:1])
         even_cols, odd_cols = pl.pallas_call(
             lambda *refs: edges(rows, *refs),
             out_shape=[jax.ShapeDtypeStruct((SLOT + 8, 128), f32)] * 2,
@@ -422,26 +434,28 @@
         )(low, high, even_rows, odd_rows, totals)
         even_cols = lax.ppermute(even_cols, COLS, swaps(cols, 0))
         odd_cols = lax.ppermute(odd_cols, COLS, swaps(cols, 1))
-        totals = add(totals + even_cols[SLOT:], gx[:2] + gy + gx[2:])
-        rest, field = pl.pallas_call(
+        totals = add(totals + even_cols[SLOT:], gy[1:] + gx[:2])
+        rest = pl.pallas_call(
             lambda *refs: collapse(rows, cols, *refs),
-            out_shape=[tile, tile],
+            out_shape=tile,
             in_specs=[vmem] * 14,
-            out_specs=[vmem] * 2,
+            out_specs=vmem,
             scratch_shapes=[pltpu.VMEM((R[1], TILE), f32), pltpu.VMEM((W[0] // 128, TILE, 128), f32)]
             + [pltpu.VMEM((2, W[1] // 128, R[1], 128), f32)],
             compiler_params=params,
             name="collapse",
         )(gains, *levels, even_rows, odd_rows, even_cols, odd_cols, wider, last, shifted)
+        totals, rest = lax.optimization_barrier((totals, rest))
+        totals = add(totals, gx[2:])
         return pl.pallas_call(
             finish,
             out_shape=tile,
-            in_specs=[vmem] * 3,
+            in_specs=[vmem] * 4,
             out_specs=pl.BlockSpec(memory_space=pl.ANY),
             scratch_shapes=[pltpu.VMEM((TILE, TILE), f32), pltpu.SemaphoreType.DMA((PARTS,))],
             compiler_params=params,
             name="finish",
-        )(rest, field, totals)
+        )(rest, ups, downs, totals)
 
     spec = P(ROWS, COLS)
     return jax.shard_map(

time: 47.4 us -> 43 us (0.907)
  waiting for transfers between devices: 16.5 us -> 10.3 us
  starting transfers between devices: 19.9 us -> 21.8 us
  local copies, waits for them, and re-layouts: 1.34 us -> 0.01 us
  other arithmetic: 0.1 us -> 0.8 us
  Pallas kernels: 9.25 us -> 9.82 us
    ppermute x6, waiting for transfers between devices: 16.5 us -> 10.3 us  [add(): totals = totals + lax.ppermute(totals, axis, pairs)]
    ppermute x6, starting transfers between devices: 11.7 us -> 14.5 us  [add(): totals = totals + lax.ppermute(totals, axis, pairs)]
    ppermute x1, starting transfers between devices: 1.66 us -> 0.23 us  [local(): even_rows = lax.ppermute(even_rows, ROWS, swaps(rows, 0))]
    concatenate x1 -> x2, other arithmetic: 0.07 us -> 0.77 us  [the longest x1 0.76 us: local(): tables = jnp.concatenate([offset, weight, gain])]
    broadcast_in_dim x3 -> x0, local copies, waits for them, and re-layouts: 0.66 us -> none  [the longest x2 0.66 us: row(): return jnp.pad(x, (0, 128 - x.shape[0]))[None]]
    unnamed x8 -> x4, local copies, waits for them, and re-layouts: 0.61 us -> 0.01 us
    pallas_call x3 -> x5, Pallas kernels: 9.07 us -> 9.64 us  [the longest x1 3.22 us: local(): pl.pallas_call(lambda *refs: scenes(rows, cols, *refs), out_shape=[jax.Sh...]
  transfers between devices with their start and end apart: 10 -> 10, of which waited for: 5 -> 4; matrix products, arithmetic and copies ran while one was open for 0% -> 0% of each run, Pallas kernels for 5% -> 12%
where the time goes in v3:
time: 43 us; the launch traced here: 42.9 us
  starting transfers between devices  21.8 us (51%)
  waiting for transfers between devices  10.3 us (24%)
  Pallas kernels  9.82 us (23%)
  other arithmetic  0.8 us (2%)
    ppermute x6, starting transfers between devices, add(): totals = totals + lax.ppermute(totals, axis, pairs)  14.5 us
    ppermute x6, waiting for transfers between devices, add(): totals = totals + lax.ppermute(totals, axis, pairs)  10.3 us
    ppermute x1, starting transfers between devices, local(): lax.ppermute(odd_rows, ROWS, swaps(rows, 1) + [(0, rows - 1), (rows - 1,...  4.4 us
    pallas_call x1, Pallas kernels, local(): pl.pallas_call(lambda *refs: scenes(rows, cols, *refs), out_shape=[jax.Sh...  3.22 us
    pallas_call x1, Pallas kernels, local(): pl.pallas_call(lambda *refs: pyramid(rows, cols, *refs), out_shape=[*stor...  2.54 us
    ppermute x1, starting transfers between devices, local(): odd_cols = lax.ppermute(odd_cols, COLS, swaps(cols, 1))  2.53 us
    pallas_call x1, Pallas kernels, local(): pl.pallas_call(lambda *refs: collapse(rows, cols, *refs), out_shape=tile,...  2.18 us
    pallas_call x1, Pallas kernels, local(): pl.pallas_call(finish, out_shape=tile, in_specs=[vmem] * 4, out_specs=pl....  1.14 us
  transfers between devices with their start and end apart: 10, of which 4 were waited for; matrix products, arithmetic and copies ran while one was open for 0% of the time, Pallas kernels for 12%

profile of v3, /device:TPU:32, one launch (start us, length us, event | category | flops | bytes accessed | tf_op | source)
XLA Modules:
  0.0 42.9 jit_solution(11851192270197780314)
XLA Ops:
  0.0 0.8 %pad_maximum_fusion.1.refs_2_ = f32[38]{0:T(128)S(1)} fusion(f32[6]{0:T(128)} %param.11, f32[16]{0:T(128)} %param.10, f32[16]{0:T(128)} %param.9), kind=kLoop, calls=%fused_computation.3 | loop fusion | flops 76 | bytes 304 | tf_op jit(solution)/shard_map/concatenate | solution.py:383
  0.8 3.2 %scenes.1 = (f32[560,128]{1,0:T(8,128)S(1)}, f32[560,128]{1,0:T(8,128)S(1)}, f32[560,128]{1,0:T(8,128)S(1)}, f32[560,128]{1,0:T(8,128)S(1)}, f32[560,128]{1,0:T(...) custom-call(f32[512,512]{1,0:T(8,128)} %refs_0_.1, ...), custom_call_target="tpu_custom_call" | custom-call | tf_op jit(solution)/shard_map/scenes/pallas_call | solution.py:384
  4.0 3.1 %collective-permute-start = (f32[8,128]{1,0:T(8,128)S(1)}, f32[8,128]{1,0:T(8,128)S(1)}, u32[]{:S(2)}, u32[]{:S(2)}) collective-permute-start(f32[8,128]{1,0:T(8,128)S(1)} %get-tuple-element.32), channel_id=1, source_target_pairs={{0,3},{3,0},{1,2},{2,1},{4,7},{7,4},{5,6},{6,5},{8,11},{11,8},{9,1... | collective-permute-start | bytes 12296 | tf_op jit(solution)/shard_map/ppermute | solution.py:377
  7.1 2.5 %pyramid.1 = (f32[2,3,304,128]{3,2,1,0:T(8,128)S(1)}, f32[2,2,176,128]{3,2,1,0:T(8,128)S(1)}, f32[2,1,112,128]{3,2,1,0:T(8,128)S(1)}, f32[2,1,80,128]{3,2,1,0:T(...) custom-call(f32[560,128]{1,0:T(8,128)S(1)} %get-tuple-element.33.ref, ...), custom_call_target="tpu_custom_call" | custom-call | tf_op jit(solution)/shard_map/pyramid/pallas_call | solution.py:402
  9.6 0.0 collective-permute-done
  9.7 0.2 collective-permute-start.1
  9.9 4.4 %collective-permute-start.3 = (f32[8,1152]{1,0:T(8,128)S(1)}, f32[8,1152]{1,0:T(8,128)S(1)}, u32[]{:S(2)}, u32[]{:S(2)}) collective-permute-start(f32[8,1152]{1,0:T(8,128)S(1)} %get-tuple-element.50), channel_id=1, source_target_pairs={{1,2},{2,1},{3,4},{4,3},{5,6},{6,5},{7,8},{8,7},{9,10},{10,9},{11,... | collective-permute-start | bytes 110600 | tf_op jit(solution)/shard_map/ppermute | solution.py:424
  14.3 0.0 collective-permute-done.1.refs_2_.refs_7_
  14.3 0.9 %collective-permute-start.2 = (f32[8,128]{1,0:T(8,128)S(1)}, f32[8,128]{1,0:T(8,128)S(1)}, u32[]{:S(2)}, u32[]{:S(2)}) collective-permute-start(f32[8,128]{1,0:T(8,128)S(1)} %slice_add_fusion.1), channel_id=1, source_target_pairs={{0,4},{4,0},{8,12},{12,8},{1,5},{5,1},{9,13},{13,9},{2,6},{6,2},{1... | collective-permute-start | bytes 12296 | tf_op jit(solution)/shard_map/ppermute | solution.py:377
  15.3 0.6 %pack.1 = (f32[80,128]{1,0:T(8,128)S(1)}, f32[80,128]{1,0:T(8,128)S(1)}) custom-call(f32[2,3,304,128]{3,2,1,0:T(8,128)S(1)} %get-tuple-element.42.refs_0_.refs_1_, f32[2,2,176,128]{3,2,1,0:T(8,128)S(1)} %get-tuple-element.43.refs_1_.refs_2_, f32[2,1,112,128]{3,2,1,0:T(8,128)S(1)} %get-tuple-element.44.refs_2_.refs_3_, ...), custom_call_target="tpu_custom_call" | custom-call | tf_op jit(solution)/shard_map/pack/pallas_call | solution.py:414
  15.8 0.0 copy-start.1
  15.8 2.1 %collective-permute-done.2 = f32[8,128]{1,0:T(8,128)S(1)} collective-permute-done((f32[8,128]{1,0:T(8,128)S(1)}, f32[8,128]{1,0:T(8,128)S(1)}, u32[]{:S(2)}, u32[]{:S(2)}) %collective-permute-start.2) | collective-permute-done | bytes 4128 | tf_op jit(solution)/shard_map/ppermute | solution.py:377
  17.9 0.0 collective-permute-done.3.refs_3_.refs_8_
  17.9 0.2 edges.1
  18.1 0.1 collective-permute-start.4
  18.2 2.5 %collective-permute-start.8 = (f32[88,128]{1,0:T(8,128)S(1)}, f32[88,128]{1,0:T(8,128)S(1)}, u32[]{:S(2)}, u32[]{:S(2)}) collective-permute-start(f32[88,128]{1,0:T(8,128)S(1)} %get-tuple-element.53), channel_id=1, source_target_pairs={{16,32},{32,16},{48,64},{64,48},{80,96},{96,80},{112,128},{128,112... | collective-permute-start | bytes 135176 | tf_op jit(solution)/shard_map/ppermute | solution.py:436
  20.8 1.9 %collective-permute-start.5 = (f32[8,128]{1,0:T(8,128)S(1)}, f32[8,128]{1,0:T(8,128)S(1)}, u32[]{:S(2)}, u32[]{:S(2)}) collective-permute-start(f32[8,128]{1,0:T(8,128)S(1)} %slice_add_fusion), channel_id=1, source_target_pairs={{0,12},{12,0},{4,8},{8,4},{1,13},{13,1},{5,9},{9,5},{2,14},{14,2},... | collective-permute-start | bytes 12296 | tf_op jit(solution)/shard_map/ppermute | solution.py:377
  22.6 3.0 %collective-permute-done.5 = f32[8,128]{1,0:T(8,128)S(1)} collective-permute-done((f32[8,128]{1,0:T(8,128)S(1)}, f32[8,128]{1,0:T(8,128)S(1)}, u32[]{:S(2)}, u32[]{:S(2)}) %collective-permute-start.5) | collective-permute-done | bytes 4128 | tf_op jit(solution)/shard_map/ppermute | solution.py:377
  25.7 3.6 %collective-permute-done.6 = f32[8,128]{1,0:T(8,128)S(1)} collective-permute-done((f32[8,128]{1,0:T(8,128)S(1)}, f32[8,128]{1,0:T(8,128)S(1)}, u32[]{:S(2)}, u32[]{:S(2)}) %collective-permute-start.6) | collective-permute-done | bytes 4128 | tf_op jit(solution)/shard_map/ppermute | solution.py:377
  29.3 2.8 %collective-permute-start.7 = (f32[8,128]{1,0:T(8,128)S(1)}, f32[8,128]{1,0:T(8,128)S(1)}, u32[]{:S(2)}, u32[]{:S(2)}) collective-permute-start(f32[8,128]{1,0:T(8,128)S(1)} %add.29), channel_id=1, source_target_pairs={{0,64},{16,80},{64,0},{80,16},{32,96},{48,112},{96,32},{112,48},{1... | collective-permute-start | bytes 12296 | tf_op jit(solution)/shard_map/ppermute | solution.py:377
  32.1 2.2 %collapse.1.rest = f32[512,512]{1,0:T(8,128)S(1)} custom-call(f32[8,128]{1,0:T(8,128)S(1)} %get-tuple-element.52.refs_0_, f32[2,3,304,128]{3,2,1,0:T(8,128)S(1)} %get-tuple-element.42.refs_0_.refs_1_, f32[2,2,176,128]{3,2,1,0:T(8,128)S(1)} %get-tuple-element.43.refs_1_.refs_2_, f32[2,1,112,128]{3,2,1,0:T(8,128)S(1)} %get-tuple-element.44.refs_2_.refs_3_, ...), custom_call_target="tpu_custom_call" | custom-call | tf_op jit(solution)/shard_map/collapse/pallas_call | solution.py:438
  34.4 5.8 %collective-permute-start.9 = (f32[8,128]{1,0:T(8,128)S(1)}, f32[8,128]{1,0:T(8,128)S(1)}, u32[]{:S(2)}, u32[]{:S(2)}) collective-permute-start(f32[8,128]{1,0:T(8,128)S(1)} %add.30), channel_id=1, source_target_pairs={{0,224},{16,240},{224,0},{240,16},{32,192},{48,208},{192,32},{208,... | collective-permute-start | bytes 12296 | tf_op jit(solution)/shard_map/ppermute | solution.py:377
  40.1 1.6 %collective-permute-done.9 = f32[8,128]{1,0:T(8,128)S(1)} collective-permute-done((f32[8,128]{1,0:T(8,128)S(1)}, f32[8,128]{1,0:T(8,128)S(1)}, u32[]{:S(2)}, u32[]{:S(2)}) %collective-permute-start.9) | collective-permute-done | bytes 4128 | tf_op jit(solution)/shard_map/ppermute | solution.py:377
  41.7 1.1 %finish.1 = f32[512,512]{1,0:T(8,128)} custom-call(f32[512,512]{1,0:T(8,128)S(1)} %collapse.1.rest, f32[512,128]{1,0:T(8,128)S(1)} %get-tuple-element.56.ups, f32[8,512]{1,0:T(8,128)S(1)} %get-tuple-element.57.downs, f32[8,128]{1,0:T(8,128)S(1)} %add.31.totals), custom_call_target="tpu_custom_call" | custom-call | tf_op jit(solution)/shard_map/finish/pallas_call | solution.py:450
  (16 shorter events, 0.1 us)
Async XLA Ops:
  4.0 5.6 %collective-permute-start = (f32[8,128]{1,0:T(8,128)S(1)}, f32[8,128]{1,0:T(8,128)S(1)}, u32[]{:S(2)}, u32[]{:S(2)}) collective-permute-start(f32[8,128]{1,0:T(8,128)S(1)} %get-tuple-element.32), channel_id=1, source_target_pairs={{0,3},{3,0},{1,2},{2,1},{4,7},{7,4},{5,6},{6,5},{8,11},{11,8},{9,1... | collective-permute-start | bytes 12296 | tf_op jit(solution)/shard_map/ppermute | solution.py:377
  9.7 4.6 %collective-permute-start.1 = (f32[8,1280]{1,0:T(8,128)S(1)}, f32[8,1280]{1,0:T(8,128)S(1)}, u32[]{:S(2)}, u32[]{:S(2)}) collective-permute-start(f32[8,1280]{1,0:T(8,128)S(1)} %pad_maximum_fusion), channel_id=1, source_target_pairs={{0,1},{1,0},{2,3},{3,2},{4,5},{5,4},{6,7},{7,6},{8,9},{9,8},{10,11... | collective-permute-start | bytes 122888 | tf_op jit(solution)/shard_map/ppermute | solution.py:423
  9.9 8.0 %collective-permute-start.3 = (f32[8,1152]{1,0:T(8,128)S(1)}, f32[8,1152]{1,0:T(8,128)S(1)}, u32[]{:S(2)}, u32[]{:S(2)}) collective-permute-start(f32[8,1152]{1,0:T(8,128)S(1)} %get-tuple-element.50), channel_id=1, source_target_pairs={{1,2},{2,1},{3,4},{4,3},{5,6},{6,5},{7,8},{8,7},{9,10},{10,9},{11,... | collective-permute-start | bytes 110600 | tf_op jit(solution)/shard_map/ppermute | solution.py:424
  14.3 3.6 %collective-permute-start.2 = (f32[8,128]{1,0:T(8,128)S(1)}, f32[8,128]{1,0:T(8,128)S(1)}, u32[]{:S(2)}, u32[]{:S(2)}) collective-permute-start(f32[8,128]{1,0:T(8,128)S(1)} %slice_add_fusion.1), channel_id=1, source_target_pairs={{0,4},{4,0},{8,12},{12,8},{1,5},{5,1},{9,13},{13,9},{2,6},{6,2},{1... | collective-permute-start | bytes 12296 | tf_op jit(solution)/shard_map/ppermute | solution.py:377
  15.3 16.9 %copy-start = (bf16[384,512]{1,0:T(8,128)(2,1)S(1)}, bf16[384,512]{1,0:T(8,128)(2,1)}, u32[]{:S(2)}) copy-start(bf16[384,512]{1,0:T(8,128)(2,1)} %constant.5.clone.refs_12_) | copy-start | bytes 1179652
  15.8 16.3 %copy-start.1 = (bf16[256,384]{1,0:T(8,128)(2,1)S(1)}, bf16[256,384]{1,0:T(8,128)(2,1)}, u32[]{:S(2)}) copy-start(bf16[256,384]{1,0:T(8,128)(2,1)} %constant.4.clone.refs_11_) | copy-start | bytes 589828
  18.1 2.6 %collective-permute-start.4 = (f32[88,128]{1,0:T(8,128)S(1)}, f32[88,128]{1,0:T(8,128)S(1)}, u32[]{:S(2)}, u32[]{:S(2)}) collective-permute-start(f32[88,128]{1,0:T(8,128)S(1)} %get-tuple-element.51), channel_id=1, source_target_pairs={{0,16},{16,0},{32,48},{48,32},{64,80},{80,64},{96,112},{112,96},{1... | collective-permute-start | bytes 135176 | tf_op jit(solution)/shard_map/ppermute | solution.py:435
  18.2 13.9 %collective-permute-start.8 = (f32[88,128]{1,0:T(8,128)S(1)}, f32[88,128]{1,0:T(8,128)S(1)}, u32[]{:S(2)}, u32[]{:S(2)}) collective-permute-start(f32[88,128]{1,0:T(8,128)S(1)} %get-tuple-element.53), channel_id=1, source_target_pairs={{16,32},{32,16},{48,64},{64,48},{80,96},{96,80},{112,128},{128,112... | collective-permute-start | bytes 135176 | tf_op jit(solution)/shard_map/ppermute | solution.py:436
  20.8 4.9 %collective-permute-start.5 = (f32[8,128]{1,0:T(8,128)S(1)}, f32[8,128]{1,0:T(8,128)S(1)}, u32[]{:S(2)}, u32[]{:S(2)}) collective-permute-start(f32[8,128]{1,0:T(8,128)S(1)} %slice_add_fusion), channel_id=1, source_target_pairs={{0,12},{12,0},{4,8},{8,4},{1,13},{13,1},{5,9},{9,5},{2,14},{14,2},... | collective-permute-start | bytes 12296 | tf_op jit(solution)/shard_map/ppermute | solution.py:377
  25.7 3.6 %collective-permute-start.6 = (f32[8,128]{1,0:T(8,128)S(1)}, f32[8,128]{1,0:T(8,128)S(1)}, u32[]{:S(2)}, u32[]{:S(2)}) collective-permute-start(f32[8,128]{1,0:T(8,128)S(1)} %add.28), channel_id=1, source_target_pairs={{0,32},{16,48},{32,0},{48,16},{64,96},{80,112},{96,64},{112,80},{1... | collective-permute-start | bytes 12296 | tf_op jit(solution)/shard_map/ppermute | solution.py:377
  29.3 5.0 %collective-permute-start.7 = (f32[8,128]{1,0:T(8,128)S(1)}, f32[8,128]{1,0:T(8,128)S(1)}, u32[]{:S(2)}, u32[]{:S(2)}) collective-permute-start(f32[8,128]{1,0:T(8,128)S(1)} %add.29), channel_id=1, source_target_pairs={{0,64},{16,80},{64,0},{80,16},{32,96},{48,112},{96,32},{112,48},{1... | collective-permute-start | bytes 12296 | tf_op jit(solution)/shard_map/ppermute | solution.py:377
  34.4 7.3 %collective-permute-start.9 = (f32[8,128]{1,0:T(8,128)S(1)}, f32[8,128]{1,0:T(8,128)S(1)}, u32[]{:S(2)}, u32[]{:S(2)}) collective-permute-start(f32[8,128]{1,0:T(8,128)S(1)} %add.30), channel_id=1, source_target_pairs={{0,224},{16,240},{224,0},{240,16},{32,192},{48,208},{192,32},{208,... | collective-permute-start | bytes 12296 | tf_op jit(solution)/shard_map/ppermute | solution.py:377

commit v4 on v3

--- a/solution.py
+++ b/solution.py
@@ -35,6 +35,7 @@
 HIGH = [0, 256, 128, 0, 0, 0, 0]
 TURN = [0, 0, 0, 64, 96, 112, 120]
 PARTS = 4
+BIG = 11
 VMEM = 40 * 1024 * 1024
 FIRST_VMEM = 50 * 1024 * 1024
 
@@ -152,7 +153,9 @@
                 ]
             return values[0]
 
-        w = lookup(SCENES)
+        tiles = [which[:, 128 * t : 128 * t + 128] for t in range(W[0] // 128)]
+        tiles = [jnp.take_along_axis(weights, t, axis=1, mode="promise_in_bounds") for t in tiles]
+        w = jnp.concatenate(tiles, axis=1)
         h = heights[at, :] + lookup(0)
         shifted[at, :] = h
         up = ups[at, :]
@@ -166,6 +169,10 @@
         return tuple(out)
 
     copies[0].wait()
+    lane = lax.broadcasted_iota(jnp.int32, (step, 128), 1)
+    weights = jnp.zeros((step, 128), jnp.float32)
+    for s in range(SCENES):
+        weights = jnp.where(lane == s, table[SCENES + s], weights)
     sums = (jnp.zeros((8, TILE), jnp.float32),) * 2
     for k in range(PARTS):
         copies[1 + 2 * k].wait()
@@ -196,7 +203,12 @@
             else:
                 taps = [load(levels[level - 2], arr, at) for at in places]
             tall = KERN[0] * (taps[0] + taps[4]) + KERN[1] * (taps[1] + taps[3]) + KERN[2] * taps[2]
-            part = jnp.where(mask, times(tall, matrix), 0.0)
+            if level == 1:
+                part = [times(tall, matrix[:, 0:256]), times(tall[:, 384:512], matrix[384:512, 256:384])]
+                part = jnp.concatenate(part, axis=1)
+            else:
+                part = times(tall, matrix)
+            part = jnp.where(mask, part, 0.0)
             store(target, arr, slice(0, 8), jnp.zeros((8, W[level]), jnp.float32))
             store(target, arr, slice(8, 8 + size), part)
             if A[level] > 8 + size:
@@ -262,7 +274,6 @@
     even_cols[0:SLOT, :] = jnp.where(even, two, one)
     odd_cols[0:SLOT, :] = jnp.where(even, one, two)
     even_cols[SLOT:, :] = totals[...]
-    odd_cols[SLOT:, :] = totals[...]
 
 
 def collapse(rows, cols, gains, l1, l2, l3, l4, l5, l6, even_rows, odd_rows, even_cols, odd_cols, wider, last, shifted, out, tall, wide, full):
@@ -312,7 +323,8 @@
         grown = jnp.concatenate([wide[tile, 0:size, :] for tile in range(W[level] // 128)], axis=1)
         change = gain[level] - gain[level - 1]
         piece = jnp.where(mask, change * value + grown, 0.0)
-    tall[...] = times(piece, last[...])
+    tall[:, 0:256] = times(piece[:, 0:256], last[0:256, 0:256])
+    tall[:, 256:512] = times(piece[:, 128:384], last[128:384, 256:512])
     half = TILE // 2
     for tile in range(W[0] // 128):
         lanes = slice(128 * tile, 128 * tile + 128)
@@ -421,11 +433,11 @@
         )(*levels)
         even_rows = jnp.concatenate([even_rows, totals], axis=1)
         even_rows = lax.ppermute(even_rows, ROWS, swaps(rows, 0))
-        odd_rows = lax.ppermute(odd_rows, ROWS, swaps(rows, 1) + [(0, rows - 1), (rows - 1, 0)])
+        odd_rows = lax.ppermute(odd_rows, ROWS, swaps(rows, 1))
         totals = add(totals + even_rows[:, STRIPS:], gy[:1])
         even_cols, odd_cols = pl.pallas_call(
             lambda *refs: edges(rows, *refs),
-            out_shape=[jax.ShapeDtypeStruct((SLOT + 8, 128), f32)] * 2,
+            out_shape=[jax.ShapeDtypeStruct((SLOT + 8, 128), f32), block],
             in_specs=[vmem] * 5,
             out_specs=[vmem] * 2,
             scratch_shapes=[pltpu.VMEM((SLOT, 128), f32)] * 2,
@@ -433,8 +445,11 @@
             name="edges",
         )(low, high, even_rows, odd_rows, totals)
         even_cols = lax.ppermute(even_cols, COLS, swaps(cols, 0))
+        totals, odd_cols = lax.optimization_barrier((totals + even_cols[SLOT:], odd_cols))
+        for axis, pairs in gx[:1]:
+            totals = totals + lax.ppermute(jnp.tile(totals, (BIG, 1)), axis, pairs)[0:8]
+        totals = add(totals, gx[1:2] + gy[1:])
         odd_cols = lax.ppermute(odd_cols, COLS, swaps(cols, 1))
-        totals = add(totals + even_cols[SLOT:], gy[1:] + gx[:2])
         rest = pl.pallas_call(
             lambda *refs: collapse(rows, cols, *refs),
             out_shape=tile,

time: 43 us -> 41.6 us (0.967)
  waiting for transfers between devices: 10.3 us -> 9.57 us
  Pallas kernels: 9.82 us -> 9.34 us
    ppermute x6 -> x5, waiting for transfers between devices: 10.3 us -> 4.44 us  [add(): totals = totals + lax.ppermute(totals, axis, pairs)]
    ppermute x1, waiting for transfers between devices: 0.01 us -> 3.2 us  [local(): even_rows = lax.ppermute(even_rows, ROWS, swaps(rows, 0))]
    ppermute x6 -> x5, starting transfers between devices: 14.5 us -> 17.3 us  [add(): totals = totals + lax.ppermute(totals, axis, pairs)]
    ppermute x1 -> x2, starting transfers between devices: 4.4 us -> 1.83 us  [the longest x1 1.18 us: local(): totals = totals + lax.ppermute(jnp.tile(totals, (BIG, 1)), axis, pairs)[0:8]]
    ppermute x1, waiting for transfers between devices: 0.01 us -> 1.21 us  [local(): even_cols = lax.ppermute(even_cols, COLS, swaps(cols, 0))]
    ppermute x1 -> x2, waiting for transfers between devices: 0.01 us -> 0.71 us  [the longest x1 0.71 us: local(): totals = totals + lax.ppermute(jnp.tile(totals, (BIG, 1)), axis, pairs)[0:8]]
  transfers between devices with their start and end apart: 10 -> 10, of which waited for: 4 -> 6; matrix products, arithmetic and copies ran while one was open for 0% -> 0% of each run, Pallas kernels for 12% -> 12%
where the time goes in v4:
time: 41.6 us; the launch traced here: 41.5 us
  starting transfers between devices  21.7 us (52%)
  waiting for transfers between devices  9.57 us (23%)
  Pallas kernels  9.34 us (22%)
  other arithmetic  0.8 us (2%)
    ppermute x5, starting transfers between devices, add(): totals = totals + lax.ppermute(totals, axis, pairs)  17.3 us
    ppermute x5, waiting for transfers between devices, add(): totals = totals + lax.ppermute(totals, axis, pairs)  4.44 us
    ppermute x1, waiting for transfers between devices, local(): even_rows = lax.ppermute(even_rows, ROWS, swaps(rows, 0))  3.2 us
    pallas_call x1, Pallas kernels, local(): pl.pallas_call(lambda *refs: scenes(rows, cols, *refs), out_shape=[jax.Sh...  3.11 us
    pallas_call x1, Pallas kernels, local(): pl.pallas_call(lambda *refs: pyramid(rows, cols, *refs), out_shape=[*stor...  2.28 us
    ppermute x1, starting transfers between devices, local(): odd_cols = lax.ppermute(odd_cols, COLS, swaps(cols, 1))  2.23 us
    pallas_call x1, Pallas kernels, local(): pl.pallas_call(lambda *refs: collapse(rows, cols, *refs), out_shape=tile,...  2.07 us
    ppermute x1, waiting for transfers between devices, local(): even_cols = lax.ppermute(even_cols, COLS, swaps(cols, 0))  1.21 us
  transfers between devices with their start and end apart: 10, of which 6 were waited for; matrix products, arithmetic and copies ran while one was open for 0% of the time, Pallas kernels for 12%

profile of v4, /device:TPU:32, one launch (start us, length us, event | category | flops | bytes accessed | tf_op | source)
XLA Modules:
  0.0 41.5 jit_solution(7845965780456592482)
XLA Ops:
  0.0 0.8 %pad_maximum_fusion.1.refs_2_ = f32[38]{0:T(128)S(1)} fusion(f32[6]{0:T(128)} %param.11, f32[16]{0:T(128)} %param.10, f32[16]{0:T(128)} %param.9), kind=kLoop, calls=%fused_computation.5 | loop fusion | flops 76 | bytes 304 | tf_op jit(solution)/shard_map/concatenate | solution.py:395
  0.8 3.1 %scenes.1 = (f32[560,128]{1,0:T(8,128)S(1)}, f32[560,128]{1,0:T(8,128)S(1)}, f32[560,128]{1,0:T(8,128)S(1)}, f32[560,128]{1,0:T(8,128)S(1)}, f32[560,128]{1,0:T(...) custom-call(f32[512,512]{1,0:T(8,128)} %refs_0_.1, ...), custom_call_target="tpu_custom_call" | custom-call | tf_op jit(solution)/shard_map/scenes/pallas_call | solution.py:396
  3.9 3.1 %collective-permute-start = (f32[8,128]{1,0:T(8,128)S(1)}, f32[8,128]{1,0:T(8,128)S(1)}, u32[]{:S(2)}, u32[]{:S(2)}) collective-permute-start(f32[8,128]{1,0:T(8,128)S(1)} %get-tuple-element.34), channel_id=1, source_target_pairs={{0,3},{3,0},{1,2},{2,1},{4,7},{7,4},{5,6},{6,5},{8,11},{11,8},{9,1... | collective-permute-start | bytes 12296 | tf_op jit(solution)/shard_map/ppermute | solution.py:389
  7.0 2.3 %pyramid.1 = (f32[2,3,304,128]{3,2,1,0:T(8,128)S(1)}, f32[2,2,176,128]{3,2,1,0:T(8,128)S(1)}, f32[2,1,112,128]{3,2,1,0:T(8,128)S(1)}, f32[2,1,80,128]{3,2,1,0:T(...) custom-call(f32[560,128]{1,0:T(8,128)S(1)} %get-tuple-element.35.ref, ...), custom_call_target="tpu_custom_call" | custom-call | tf_op jit(solution)/shard_map/pyramid/pallas_call | solution.py:414
  9.3 0.2 collective-permute-start.1
  9.5 0.7 %collective-permute-start.3 = (f32[8,1152]{1,0:T(8,128)S(1)}, f32[8,1152]{1,0:T(8,128)S(1)}, u32[]{:S(2)}, u32[]{:S(2)}) collective-permute-start(f32[8,1152]{1,0:T(8,128)S(1)} %get-tuple-element.52), channel_id=1, source_target_pairs={{1,2},{2,1},{3,4},{4,3},{5,6},{6,5},{7,8},{8,7},{9,10},{10,9},{11,... | collective-permute-start | bytes 110600 | tf_op jit(solution)/shard_map/ppermute | solution.py:436
  10.2 3.2 %collective-permute-done.1.refs_2_.refs_7_ = f32[8,1280]{1,0:T(8,128)S(1)} collective-permute-done((f32[8,1280]{1,0:T(8,128)S(1)}, f32[8,1280]{1,0:T(8,128)S(1)}, u32[]{:S(2)}, u32[]{:S(2)}) %collective-permute-start.1) | collective-permute-done | bytes 40992 | tf_op jit(solution)/shard_map/ppermute | solution.py:435
  13.4 2.0 %collective-permute-start.2 = (f32[8,128]{1,0:T(8,128)S(1)}, f32[8,128]{1,0:T(8,128)S(1)}, u32[]{:S(2)}, u32[]{:S(2)}) collective-permute-start(f32[8,128]{1,0:T(8,128)S(1)} %slice_add_fusion.2), channel_id=1, source_target_pairs={{0,4},{4,0},{8,12},{12,8},{1,5},{5,1},{9,13},{13,9},{2,6},{6,2},{1... | collective-permute-start | bytes 12296 | tf_op jit(solution)/shard_map/ppermute | solution.py:389
  15.4 0.6 %pack.1 = (f32[80,128]{1,0:T(8,128)S(1)}, f32[80,128]{1,0:T(8,128)S(1)}) custom-call(f32[2,3,304,128]{3,2,1,0:T(8,128)S(1)} %get-tuple-element.44.refs_0_.refs_1_, f32[2,2,176,128]{3,2,1,0:T(8,128)S(1)} %get-tuple-element.45.refs_1_.refs_2_, f32[2,1,112,128]{3,2,1,0:T(8,128)S(1)} %get-tuple-element.46.refs_2_.refs_3_, ...), custom_call_target="tpu_custom_call" | custom-call | tf_op jit(solution)/shard_map/pack/pallas_call | solution.py:426
  16.0 0.0 copy-start.1
  16.0 1.3 %collective-permute-done.2 = f32[8,128]{1,0:T(8,128)S(1)} collective-permute-done((f32[8,128]{1,0:T(8,128)S(1)}, f32[8,128]{1,0:T(8,128)S(1)}, u32[]{:S(2)}, u32[]{:S(2)}) %collective-permute-start.2) | collective-permute-done | bytes 4128 | tf_op jit(solution)/shard_map/ppermute | solution.py:389
  17.2 0.2 edges.1
  17.4 0.1 collective-permute-start.4
  17.5 1.2 %collective-permute-done.4.refs_9_ = f32[88,128]{1,0:T(8,128)S(1)} collective-permute-done((f32[88,128]{1,0:T(8,128)S(1)}, f32[88,128]{1,0:T(8,128)S(1)}, u32[]{:S(2)}, u32[]{:S(2)}) %collective-permute-start.4) | collective-permute-done | bytes 45088 | tf_op jit(solution)/shard_map/ppermute | solution.py:447
  18.8 1.2 %collective-permute-start.5 = (f32[88,128]{1,0:T(8,128)S(1)}, f32[88,128]{1,0:T(8,128)S(1)}, u32[]{:S(2)}, u32[]{:S(2)}) collective-permute-start(f32[88,128]{1,0:T(8,128)S(1)} %broadcast_bitcast_fusion), channel_id=1, source_target_pairs={{0,32},{16,48},{32,0},{48,16},{64,96},{80,112},{96,64},{112,80},{1... | collective-permute-start | bytes 135176 | tf_op jit(solution)/shard_map/ppermute | solution.py:450
  19.9 2.2 %collective-permute-start.8 = (f32[80,128]{1,0:T(8,128)S(1)}, f32[80,128]{1,0:T(8,128)S(1)}, u32[]{:S(2)}, u32[]{:S(2)}) collective-permute-start(f32[80,128]{1,0:T(8,128)S(1)} %get-tuple-element.57), channel_id=1, source_target_pairs={{16,32},{32,16},{48,64},{64,48},{80,96},{96,80},{112,128},{128,112... | collective-permute-start | bytes 122888 | tf_op jit(solution)/shard_map/ppermute | solution.py:452
  22.2 0.7 %collective-permute-done.5 = f32[88,128]{1,0:T(8,128)S(1)} collective-permute-done((f32[88,128]{1,0:T(8,128)S(1)}, f32[88,128]{1,0:T(8,128)S(1)}, u32[]{:S(2)}, u32[]{:S(2)}) %collective-permute-start.5) | collective-permute-done | bytes 45088 | tf_op jit(solution)/shard_map/ppermute | solution.py:450
  22.9 3.3 %collective-permute-start.6 = (f32[8,128]{1,0:T(8,128)S(1)}, f32[8,128]{1,0:T(8,128)S(1)}, u32[]{:S(2)}, u32[]{:S(2)}) collective-permute-start(f32[8,128]{1,0:T(8,128)S(1)} %slice_add_fusion), channel_id=1, source_target_pairs={{0,64},{16,80},{64,0},{80,16},{32,96},{48,112},{96,32},{112,48},{1... | collective-permute-start | bytes 12296 | tf_op jit(solution)/shard_map/ppermute | solution.py:389
  26.1 1.6 %collective-permute-done.6 = f32[8,128]{1,0:T(8,128)S(1)} collective-permute-done((f32[8,128]{1,0:T(8,128)S(1)}, f32[8,128]{1,0:T(8,128)S(1)}, u32[]{:S(2)}, u32[]{:S(2)}) %collective-permute-start.6) | collective-permute-done | bytes 4128 | tf_op jit(solution)/shard_map/ppermute | solution.py:389
  27.7 3.3 %collective-permute-start.7 = (f32[8,128]{1,0:T(8,128)S(1)}, f32[8,128]{1,0:T(8,128)S(1)}, u32[]{:S(2)}, u32[]{:S(2)}) collective-permute-start(f32[8,128]{1,0:T(8,128)S(1)} %add.29), channel_id=1, source_target_pairs={{0,12},{12,0},{4,8},{8,4},{1,13},{13,1},{5,9},{9,5},{2,14},{14,2},... | collective-permute-start | bytes 12296 | tf_op jit(solution)/shard_map/ppermute | solution.py:389
  31.1 2.1 %collapse.1.rest = f32[512,512]{1,0:T(8,128)S(1)} custom-call(f32[8,128]{1,0:T(8,128)S(1)} %get-tuple-element.56.refs_0_, f32[2,3,304,128]{3,2,1,0:T(8,128)S(1)} %get-tuple-element.44.refs_0_.refs_1_, f32[2,2,176,128]{3,2,1,0:T(8,128)S(1)} %get-tuple-element.45.refs_1_.refs_2_, f32[2,1,112,128]{3,2,1,0:T(8,128)S(1)} %get-tuple-element.46.refs_2_.refs_3_, ...), custom_call_target="tpu_custom_call" | custom-call | tf_op jit(solution)/shard_map/collapse/pallas_call | solution.py:453
  33.2 5.6 %collective-permute-start.9 = (f32[8,128]{1,0:T(8,128)S(1)}, f32[8,128]{1,0:T(8,128)S(1)}, u32[]{:S(2)}, u32[]{:S(2)}) collective-permute-start(f32[8,128]{1,0:T(8,128)S(1)} %add.30), channel_id=1, source_target_pairs={{0,224},{16,240},{224,0},{240,16},{32,192},{48,208},{192,32},{208,... | collective-permute-start | bytes 12296 | tf_op jit(solution)/shard_map/ppermute | solution.py:389
  38.8 1.6 %collective-permute-done.9 = f32[8,128]{1,0:T(8,128)S(1)} collective-permute-done((f32[8,128]{1,0:T(8,128)S(1)}, f32[8,128]{1,0:T(8,128)S(1)}, u32[]{:S(2)}, u32[]{:S(2)}) %collective-permute-start.9) | collective-permute-done | bytes 4128 | tf_op jit(solution)/shard_map/ppermute | solution.py:389
  40.4 1.1 %finish.1 = f32[512,512]{1,0:T(8,128)} custom-call(f32[512,512]{1,0:T(8,128)S(1)} %collapse.1.rest, f32[512,128]{1,0:T(8,128)S(1)} %get-tuple-element.60.ups, f32[8,512]{1,0:T(8,128)S(1)} %get-tuple-element.61.downs, f32[8,128]{1,0:T(8,128)S(1)} %add.31.totals), custom_call_target="tpu_custom_call" | custom-call | tf_op jit(solution)/shard_map/finish/pallas_call | solution.py:465
  (17 shorter events, 0.1 us)
Async XLA Ops:
  3.9 5.4 %collective-permute-start = (f32[8,128]{1,0:T(8,128)S(1)}, f32[8,128]{1,0:T(8,128)S(1)}, u32[]{:S(2)}, u32[]{:S(2)}) collective-permute-start(f32[8,128]{1,0:T(8,128)S(1)} %get-tuple-element.34), channel_id=1, source_target_pairs={{0,3},{3,0},{1,2},{2,1},{4,7},{7,4},{5,6},{6,5},{8,11},{11,8},{9,1... | collective-permute-start | bytes 12296 | tf_op jit(solution)/shard_map/ppermute | solution.py:389
  9.3 4.1 %collective-permute-start.1 = (f32[8,1280]{1,0:T(8,128)S(1)}, f32[8,1280]{1,0:T(8,128)S(1)}, u32[]{:S(2)}, u32[]{:S(2)}) collective-permute-start(f32[8,1280]{1,0:T(8,128)S(1)} %pad_maximum_fusion), channel_id=1, source_target_pairs={{0,1},{1,0},{2,3},{3,2},{4,5},{5,4},{6,7},{7,6},{8,9},{9,8},{10,11... | collective-permute-start | bytes 122888 | tf_op jit(solution)/shard_map/ppermute | solution.py:435
  9.5 7.7 %collective-permute-start.3 = (f32[8,1152]{1,0:T(8,128)S(1)}, f32[8,1152]{1,0:T(8,128)S(1)}, u32[]{:S(2)}, u32[]{:S(2)}) collective-permute-start(f32[8,1152]{1,0:T(8,128)S(1)} %get-tuple-element.52), channel_id=1, source_target_pairs={{1,2},{2,1},{3,4},{4,3},{5,6},{6,5},{7,8},{8,7},{9,10},{10,9},{11,... | collective-permute-start | bytes 110600 | tf_op jit(solution)/shard_map/ppermute | solution.py:436
  13.4 3.8 %collective-permute-start.2 = (f32[8,128]{1,0:T(8,128)S(1)}, f32[8,128]{1,0:T(8,128)S(1)}, u32[]{:S(2)}, u32[]{:S(2)}) collective-permute-start(f32[8,128]{1,0:T(8,128)S(1)} %slice_add_fusion.2), channel_id=1, source_target_pairs={{0,4},{4,0},{8,12},{12,8},{1,5},{5,1},{9,13},{13,9},{2,6},{6,2},{1... | collective-permute-start | bytes 12296 | tf_op jit(solution)/shard_map/ppermute | solution.py:389
  15.4 15.7 %copy-start = (bf16[384,512]{1,0:T(8,128)(2,1)S(1)}, bf16[384,512]{1,0:T(8,128)(2,1)}, u32[]{:S(2)}) copy-start(bf16[384,512]{1,0:T(8,128)(2,1)} %constant.5.clone.refs_12_) | copy-start | bytes 1179652
  16.0 15.1 %copy-start.1 = (bf16[256,384]{1,0:T(8,128)(2,1)S(1)}, bf16[256,384]{1,0:T(8,128)(2,1)}, u32[]{:S(2)}) copy-start(bf16[256,384]{1,0:T(8,128)(2,1)} %constant.4.clone.refs_11_) | copy-start | bytes 589828
  17.4 1.3 %collective-permute-start.4 = (f32[88,128]{1,0:T(8,128)S(1)}, f32[88,128]{1,0:T(8,128)S(1)}, u32[]{:S(2)}, u32[]{:S(2)}) collective-permute-start(f32[88,128]{1,0:T(8,128)S(1)} %get-tuple-element.53), channel_id=1, source_target_pairs={{0,16},{16,0},{32,48},{48,32},{64,80},{80,64},{96,112},{112,96},{1... | collective-permute-start | bytes 135176 | tf_op jit(solution)/shard_map/ppermute | solution.py:447
  18.8 4.1 %collective-permute-start.5 = (f32[88,128]{1,0:T(8,128)S(1)}, f32[88,128]{1,0:T(8,128)S(1)}, u32[]{:S(2)}, u32[]{:S(2)}) collective-permute-start(f32[88,128]{1,0:T(8,128)S(1)} %broadcast_bitcast_fusion), channel_id=1, source_target_pairs={{0,32},{16,48},{32,0},{48,16},{64,96},{80,112},{96,64},{112,80},{1... | collective-permute-start | bytes 135176 | tf_op jit(solution)/shard_map/ppermute | solution.py:450
  19.9 11.1 %collective-permute-start.8 = (f32[80,128]{1,0:T(8,128)S(1)}, f32[80,128]{1,0:T(8,128)S(1)}, u32[]{:S(2)}, u32[]{:S(2)}) collective-permute-start(f32[80,128]{1,0:T(8,128)S(1)} %get-tuple-element.57), channel_id=1, source_target_pairs={{16,32},{32,16},{48,64},{64,48},{80,96},{96,80},{112,128},{128,112... | collective-permute-start | bytes 122888 | tf_op jit(solution)/shard_map/ppermute | solution.py:452
  22.9 4.9 %collective-permute-start.6 = (f32[8,128]{1,0:T(8,128)S(1)}, f32[8,128]{1,0:T(8,128)S(1)}, u32[]{:S(2)}, u32[]{:S(2)}) collective-permute-start(f32[8,128]{1,0:T(8,128)S(1)} %slice_add_fusion), channel_id=1, source_target_pairs={{0,64},{16,80},{64,0},{80,16},{32,96},{48,112},{96,32},{112,48},{1... | collective-permute-start | bytes 12296 | tf_op jit(solution)/shard_map/ppermute | solution.py:389
  27.7 5.4 %collective-permute-start.7 = (f32[8,128]{1,0:T(8,128)S(1)}, f32[8,128]{1,0:T(8,128)S(1)}, u32[]{:S(2)}, u32[]{:S(2)}) collective-permute-start(f32[8,128]{1,0:T(8,128)S(1)} %add.29), channel_id=1, source_target_pairs={{0,12},{12,0},{4,8},{8,4},{1,13},{13,1},{5,9},{9,5},{2,14},{14,2},... | collective-permute-start | bytes 12296 | tf_op jit(solution)/shard_map/ppermute | solution.py:389
  33.2 7.2 %collective-permute-start.9 = (f32[8,128]{1,0:T(8,128)S(1)}, f32[8,128]{1,0:T(8,128)S(1)}, u32[]{:S(2)}, u32[]{:S(2)}) collective-permute-start(f32[8,128]{1,0:T(8,128)S(1)} %add.30), channel_id=1, source_target_pairs={{0,224},{16,240},{224,0},{240,16},{32,192},{48,208},{192,32},{208,... | collective-permute-start | bytes 12296 | tf_op jit(solution)/shard_map/ppermute | solution.py:389

commit v5 on v4

--- a/solution.py
+++ b/solution.py
@@ -121,7 +121,7 @@
 
 def scenes(rows, cols, heights_in, ids_in, tables, *refs):
     base, (shifted, totals, gains, ups, downs, heights, ids, tall, wide, table, sems) = refs[:8], refs[8:]
-    step, part = 32, TILE // PARTS
+    step, part = 64, TILE // PARTS
     pairs = [(tables, table)]
     for k in range(PARTS):
         at = slice(k * part, k * part + part)
@@ -448,7 +448,7 @@
         totals, odd_cols = lax.optimization_barrier((totals + even_cols[SLOT:], odd_cols))
         for axis, pairs in gx[:1]:
             totals = totals + lax.ppermute(jnp.tile(totals, (BIG, 1)), axis, pairs)[0:8]
-        totals = add(totals, gx[1:2] + gy[1:])
+        totals = add(totals, gy[1:] + gx[1:2])
         odd_cols = lax.ppermute(odd_cols, COLS, swaps(cols, 1))
         rest = pl.pallas_call(
             lambda *refs: collapse(rows, cols, *refs),

time: 41.6 us -> 41.1 us (0.988); the launches traced: 41.5 us -> 40.5 us
  starting transfers between devices: 21.7 us -> 21.1 us
  Pallas kernels: 9.34 us -> 8.8 us
    ppermute x5, starting transfers between devices: 17.3 us -> 16.7 us  [add(): totals = totals + lax.ppermute(totals, axis, pairs)]
    pallas_call x1, Pallas kernels: 3.11 us -> 2.57 us  [local(): pl.pallas_call(lambda *refs: scenes(rows, cols, *refs), out_shape=[jax.Sh...]
where the time goes in v5:
time: 41.1 us; the launch traced here: 40.5 us
  starting transfers between devices  21.1 us (51%)
  waiting for transfers between devices  9.71 us (24%)
  Pallas kernels  8.8 us (21%)
  other arithmetic  0.8 us (2%)
    ppermute x5, starting transfers between devices, add(): totals = totals + lax.ppermute(totals, axis, pairs)  16.7 us
    ppermute x5, waiting for transfers between devices, add(): totals = totals + lax.ppermute(totals, axis, pairs)  4.58 us
    ppermute x1, waiting for transfers between devices, local(): even_rows = lax.ppermute(even_rows, ROWS, swaps(rows, 0))  3.2 us
    pallas_call x1, Pallas kernels, local(): pl.pallas_call(lambda *refs: scenes(rows, cols, *refs), out_shape=[jax.Sh...  2.57 us
    pallas_call x1, Pallas kernels, local(): pl.pallas_call(lambda *refs: pyramid(rows, cols, *refs), out_shape=[*stor...  2.28 us
    ppermute x1, starting transfers between devices, local(): odd_cols = lax.ppermute(odd_cols, COLS, swaps(cols, 1))  2.23 us
    pallas_call x1, Pallas kernels, local(): pl.pallas_call(lambda *refs: collapse(rows, cols, *refs), out_shape=tile,...  2.07 us
    ppermute x1, waiting for transfers between devices, local(): even_cols = lax.ppermute(even_cols, COLS, swaps(cols, 0))  1.21 us
  transfers between devices with their start and end apart: 10, of which 6 were waited for; matrix products, arithmetic and copies ran while one was open for 0% of the time, Pallas kernels for 12%

profile of v5, /device:TPU:32, one launch (start us, length us, event | category | flops | bytes accessed | tf_op | source)
XLA Modules:
  0.0 40.5 jit_solution(3216996607441058060)
XLA Ops:
  0.0 0.8 %pad_maximum_fusion.1.refs_2_ = f32[38]{0:T(128)S(1)} fusion(f32[6]{0:T(128)} %param.11, f32[16]{0:T(128)} %param.10, f32[16]{0:T(128)} %param.9), kind=kLoop, calls=%fused_computation.5 | loop fusion | flops 76 | bytes 304 | tf_op jit(solution)/shard_map/concatenate | solution.py:395
  0.8 2.6 %scenes.1 = (f32[560,128]{1,0:T(8,128)S(1)}, f32[560,128]{1,0:T(8,128)S(1)}, f32[560,128]{1,0:T(8,128)S(1)}, f32[560,128]{1,0:T(8,128)S(1)}, f32[560,128]{1,0:T(...) custom-call(f32[512,512]{1,0:T(8,128)} %refs_0_.1, ...), custom_call_target="tpu_custom_call" | custom-call | tf_op jit(solution)/shard_map/scenes/pallas_call | solution.py:396
  3.3 3.1 %collective-permute-start = (f32[8,128]{1,0:T(8,128)S(1)}, f32[8,128]{1,0:T(8,128)S(1)}, u32[]{:S(2)}, u32[]{:S(2)}) collective-permute-start(f32[8,128]{1,0:T(8,128)S(1)} %get-tuple-element.34), channel_id=1, source_target_pairs={{0,3},{3,0},{1,2},{2,1},{4,7},{7,4},{5,6},{6,5},{8,11},{11,8},{9,1... | collective-permute-start | bytes 12296 | tf_op jit(solution)/shard_map/ppermute | solution.py:389
  6.4 2.3 %pyramid.1 = (f32[2,3,304,128]{3,2,1,0:T(8,128)S(1)}, f32[2,2,176,128]{3,2,1,0:T(8,128)S(1)}, f32[2,1,112,128]{3,2,1,0:T(8,128)S(1)}, f32[2,1,80,128]{3,2,1,0:T(...) custom-call(f32[560,128]{1,0:T(8,128)S(1)} %get-tuple-element.35.ref, ...), custom_call_target="tpu_custom_call" | custom-call | tf_op jit(solution)/shard_map/pyramid/pallas_call | solution.py:414
  8.8 0.2 collective-permute-start.1
  9.0 0.7 %collective-permute-start.3 = (f32[8,1152]{1,0:T(8,128)S(1)}, f32[8,1152]{1,0:T(8,128)S(1)}, u32[]{:S(2)}, u32[]{:S(2)}) collective-permute-start(f32[8,1152]{1,0:T(8,128)S(1)} %get-tuple-element.52), channel_id=1, source_target_pairs={{1,2},{2,1},{3,4},{4,3},{5,6},{6,5},{7,8},{8,7},{9,10},{10,9},{11,... | collective-permute-start | bytes 110600 | tf_op jit(solution)/shard_map/ppermute | solution.py:436
  9.6 3.2 %collective-permute-done.1.refs_2_.refs_7_ = f32[8,1280]{1,0:T(8,128)S(1)} collective-permute-done((f32[8,1280]{1,0:T(8,128)S(1)}, f32[8,1280]{1,0:T(8,128)S(1)}, u32[]{:S(2)}, u32[]{:S(2)}) %collective-permute-start.1) | collective-permute-done | bytes 40992 | tf_op jit(solution)/shard_map/ppermute | solution.py:435
  12.9 2.0 %collective-permute-start.2 = (f32[8,128]{1,0:T(8,128)S(1)}, f32[8,128]{1,0:T(8,128)S(1)}, u32[]{:S(2)}, u32[]{:S(2)}) collective-permute-start(f32[8,128]{1,0:T(8,128)S(1)} %slice_add_fusion.2), channel_id=1, source_target_pairs={{0,4},{4,0},{8,12},{12,8},{1,5},{5,1},{9,13},{13,9},{2,6},{6,2},{1... | collective-permute-start | bytes 12296 | tf_op jit(solution)/shard_map/ppermute | solution.py:389
  14.9 0.6 %pack.1 = (f32[80,128]{1,0:T(8,128)S(1)}, f32[80,128]{1,0:T(8,128)S(1)}) custom-call(f32[2,3,304,128]{3,2,1,0:T(8,128)S(1)} %get-tuple-element.44.refs_0_.refs_1_, f32[2,2,176,128]{3,2,1,0:T(8,128)S(1)} %get-tuple-element.45.refs_1_.refs_2_, f32[2,1,112,128]{3,2,1,0:T(8,128)S(1)} %get-tuple-element.46.refs_2_.refs_3_, ...), custom_call_target="tpu_custom_call" | custom-call | tf_op jit(solution)/shard_map/pack/pallas_call | solution.py:426
  15.4 0.0 copy-start.1
  15.4 1.3 %collective-permute-done.2 = f32[8,128]{1,0:T(8,128)S(1)} collective-permute-done((f32[8,128]{1,0:T(8,128)S(1)}, f32[8,128]{1,0:T(8,128)S(1)}, u32[]{:S(2)}, u32[]{:S(2)}) %collective-permute-start.2) | collective-permute-done | bytes 4128 | tf_op jit(solution)/shard_map/ppermute | solution.py:389
  16.7 0.2 edges.1
  16.9 0.1 collective-permute-start.4
  17.0 1.2 %collective-permute-done.4.refs_9_ = f32[88,128]{1,0:T(8,128)S(1)} collective-permute-done((f32[88,128]{1,0:T(8,128)S(1)}, f32[88,128]{1,0:T(8,128)S(1)}, u32[]{:S(2)}, u32[]{:S(2)}) %collective-permute-start.4) | collective-permute-done | bytes 45088 | tf_op jit(solution)/shard_map/ppermute | solution.py:447
  18.2 1.2 %collective-permute-start.5 = (f32[88,128]{1,0:T(8,128)S(1)}, f32[88,128]{1,0:T(8,128)S(1)}, u32[]{:S(2)}, u32[]{:S(2)}) collective-permute-start(f32[88,128]{1,0:T(8,128)S(1)} %broadcast_bitcast_fusion), channel_id=1, source_target_pairs={{0,32},{16,48},{32,0},{48,16},{64,96},{80,112},{96,64},{112,80},{1... | collective-permute-start | bytes 135176 | tf_op jit(solution)/shard_map/ppermute | solution.py:450
  19.4 2.2 %collective-permute-start.8 = (f32[80,128]{1,0:T(8,128)S(1)}, f32[80,128]{1,0:T(8,128)S(1)}, u32[]{:S(2)}, u32[]{:S(2)}) collective-permute-start(f32[80,128]{1,0:T(8,128)S(1)} %get-tuple-element.57), channel_id=1, source_target_pairs={{16,32},{32,16},{48,64},{64,48},{80,96},{96,80},{112,128},{128,112... | collective-permute-start | bytes 122888 | tf_op jit(solution)/shard_map/ppermute | solution.py:452
  21.6 0.7 %collective-permute-done.5 = f32[88,128]{1,0:T(8,128)S(1)} collective-permute-done((f32[88,128]{1,0:T(8,128)S(1)}, f32[88,128]{1,0:T(8,128)S(1)}, u32[]{:S(2)}, u32[]{:S(2)}) %collective-permute-start.5) | collective-permute-done | bytes 45088 | tf_op jit(solution)/shard_map/ppermute | solution.py:450
  22.3 3.3 %collective-permute-start.6 = (f32[8,128]{1,0:T(8,128)S(1)}, f32[8,128]{1,0:T(8,128)S(1)}, u32[]{:S(2)}, u32[]{:S(2)}) collective-permute-start(f32[8,128]{1,0:T(8,128)S(1)} %slice_add_fusion), channel_id=1, source_target_pairs={{0,12},{12,0},{4,8},{8,4},{1,13},{13,1},{5,9},{9,5},{2,14},{14,2},... | collective-permute-start | bytes 12296 | tf_op jit(solution)/shard_map/ppermute | solution.py:389
  25.7 1.6 %collective-permute-done.6 = f32[8,128]{1,0:T(8,128)S(1)} collective-permute-done((f32[8,128]{1,0:T(8,128)S(1)}, f32[8,128]{1,0:T(8,128)S(1)}, u32[]{:S(2)}, u32[]{:S(2)}) %collective-permute-start.6) | collective-permute-done | bytes 4128 | tf_op jit(solution)/shard_map/ppermute | solution.py:389
  27.3 3.3 %collective-permute-start.7 = (f32[8,128]{1,0:T(8,128)S(1)}, f32[8,128]{1,0:T(8,128)S(1)}, u32[]{:S(2)}, u32[]{:S(2)}) collective-permute-start(f32[8,128]{1,0:T(8,128)S(1)} %add.29), channel_id=1, source_target_pairs={{0,64},{16,80},{64,0},{80,16},{32,96},{48,112},{96,32},{112,48},{1... | collective-permute-start | bytes 12296 | tf_op jit(solution)/shard_map/ppermute | solution.py:389
  30.5 2.1 %collapse.1.rest = f32[512,512]{1,0:T(8,128)S(1)} custom-call(f32[8,128]{1,0:T(8,128)S(1)} %get-tuple-element.56.refs_0_, f32[2,3,304,128]{3,2,1,0:T(8,128)S(1)} %get-tuple-element.44.refs_0_.refs_1_, f32[2,2,176,128]{3,2,1,0:T(8,128)S(1)} %get-tuple-element.45.refs_1_.refs_2_, f32[2,1,112,128]{3,2,1,0:T(8,128)S(1)} %get-tuple-element.46.refs_2_.refs_3_, ...), custom_call_target="tpu_custom_call" | custom-call | tf_op jit(solution)/shard_map/collapse/pallas_call | solution.py:453
  32.6 5.0 %collective-permute-start.9 = (f32[8,128]{1,0:T(8,128)S(1)}, f32[8,128]{1,0:T(8,128)S(1)}, u32[]{:S(2)}, u32[]{:S(2)}) collective-permute-start(f32[8,128]{1,0:T(8,128)S(1)} %add.30), channel_id=1, source_target_pairs={{0,224},{16,240},{224,0},{240,16},{32,192},{48,208},{192,32},{208,... | collective-permute-start | bytes 12296 | tf_op jit(solution)/shard_map/ppermute | solution.py:389
  37.6 1.7 %collective-permute-done.9 = f32[8,128]{1,0:T(8,128)S(1)} collective-permute-done((f32[8,128]{1,0:T(8,128)S(1)}, f32[8,128]{1,0:T(8,128)S(1)}, u32[]{:S(2)}, u32[]{:S(2)}) %collective-permute-start.9) | collective-permute-done | bytes 4128 | tf_op jit(solution)/shard_map/ppermute | solution.py:389
  39.3 1.1 %finish.1 = f32[512,512]{1,0:T(8,128)} custom-call(f32[512,512]{1,0:T(8,128)S(1)} %collapse.1.rest, f32[512,128]{1,0:T(8,128)S(1)} %get-tuple-element.60.ups, f32[8,512]{1,0:T(8,128)S(1)} %get-tuple-element.61.downs, f32[8,128]{1,0:T(8,128)S(1)} %add.31.totals), custom_call_target="tpu_custom_call" | custom-call | tf_op jit(solution)/shard_map/finish/pallas_call | solution.py:465
  (17 shorter events, 0.1 us)
Async XLA Ops:
  3.3 5.4 %collective-permute-start = (f32[8,128]{1,0:T(8,128)S(1)}, f32[8,128]{1,0:T(8,128)S(1)}, u32[]{:S(2)}, u32[]{:S(2)}) collective-permute-start(f32[8,128]{1,0:T(8,128)S(1)} %get-tuple-element.34), channel_id=1, source_target_pairs={{0,3},{3,0},{1,2},{2,1},{4,7},{7,4},{5,6},{6,5},{8,11},{11,8},{9,1... | collective-permute-start | bytes 12296 | tf_op jit(solution)/shard_map/ppermute | solution.py:389
  8.8 4.1 %collective-permute-start.1 = (f32[8,1280]{1,0:T(8,128)S(1)}, f32[8,1280]{1,0:T(8,128)S(1)}, u32[]{:S(2)}, u32[]{:S(2)}) collective-permute-start(f32[8,1280]{1,0:T(8,128)S(1)} %pad_maximum_fusion), channel_id=1, source_target_pairs={{0,1},{1,0},{2,3},{3,2},{4,5},{5,4},{6,7},{7,6},{8,9},{9,8},{10,11... | collective-permute-start | bytes 122888 | tf_op jit(solution)/shard_map/ppermute | solution.py:435
  9.0 7.7 %collective-permute-start.3 = (f32[8,1152]{1,0:T(8,128)S(1)}, f32[8,1152]{1,0:T(8,128)S(1)}, u32[]{:S(2)}, u32[]{:S(2)}) collective-permute-start(f32[8,1152]{1,0:T(8,128)S(1)} %get-tuple-element.52), channel_id=1, source_target_pairs={{1,2},{2,1},{3,4},{4,3},{5,6},{6,5},{7,8},{8,7},{9,10},{10,9},{11,... | collective-permute-start | bytes 110600 | tf_op jit(solution)/shard_map/ppermute | solution.py:436
  12.9 3.8 %collective-permute-start.2 = (f32[8,128]{1,0:T(8,128)S(1)}, f32[8,128]{1,0:T(8,128)S(1)}, u32[]{:S(2)}, u32[]{:S(2)}) collective-permute-start(f32[8,128]{1,0:T(8,128)S(1)} %slice_add_fusion.2), channel_id=1, source_target_pairs={{0,4},{4,0},{8,12},{12,8},{1,5},{5,1},{9,13},{13,9},{2,6},{6,2},{1... | collective-permute-start | bytes 12296 | tf_op jit(solution)/shard_map/ppermute | solution.py:389
  14.9 15.7 %copy-start = (bf16[384,512]{1,0:T(8,128)(2,1)S(1)}, bf16[384,512]{1,0:T(8,128)(2,1)}, u32[]{:S(2)}) copy-start(bf16[384,512]{1,0:T(8,128)(2,1)} %constant.5.clone.refs_12_) | copy-start | bytes 1179652
  15.4 15.1 %copy-start.1 = (bf16[256,384]{1,0:T(8,128)(2,1)S(1)}, bf16[256,384]{1,0:T(8,128)(2,1)}, u32[]{:S(2)}) copy-start(bf16[256,384]{1,0:T(8,128)(2,1)} %constant.4.clone.refs_11_) | copy-start | bytes 589828
  16.9 1.3 %collective-permute-start.4 = (f32[88,128]{1,0:T(8,128)S(1)}, f32[88,128]{1,0:T(8,128)S(1)}, u32[]{:S(2)}, u32[]{:S(2)}) collective-permute-start(f32[88,128]{1,0:T(8,128)S(1)} %get-tuple-element.53), channel_id=1, source_target_pairs={{0,16},{16,0},{32,48},{48,32},{64,80},{80,64},{96,112},{112,96},{1... | collective-permute-start | bytes 135176 | tf_op jit(solution)/shard_map/ppermute | solution.py:447
  18.2 4.1 %collective-permute-start.5 = (f32[88,128]{1,0:T(8,128)S(1)}, f32[88,128]{1,0:T(8,128)S(1)}, u32[]{:S(2)}, u32[]{:S(2)}) collective-permute-start(f32[88,128]{1,0:T(8,128)S(1)} %broadcast_bitcast_fusion), channel_id=1, source_target_pairs={{0,32},{16,48},{32,0},{48,16},{64,96},{80,112},{96,64},{112,80},{1... | collective-permute-start | bytes 135176 | tf_op jit(solution)/shard_map/ppermute | solution.py:450
  19.4 11.1 %collective-permute-start.8 = (f32[80,128]{1,0:T(8,128)S(1)}, f32[80,128]{1,0:T(8,128)S(1)}, u32[]{:S(2)}, u32[]{:S(2)}) collective-permute-start(f32[80,128]{1,0:T(8,128)S(1)} %get-tuple-element.57), channel_id=1, source_target_pairs={{16,32},{32,16},{48,64},{64,48},{80,96},{96,80},{112,128},{128,112... | collective-permute-start | bytes 122888 | tf_op jit(solution)/shard_map/ppermute | solution.py:452
  22.3 4.9 %collective-permute-start.6 = (f32[8,128]{1,0:T(8,128)S(1)}, f32[8,128]{1,0:T(8,128)S(1)}, u32[]{:S(2)}, u32[]{:S(2)}) collective-permute-start(f32[8,128]{1,0:T(8,128)S(1)} %slice_add_fusion), channel_id=1, source_target_pairs={{0,12},{12,0},{4,8},{8,4},{1,13},{13,1},{5,9},{9,5},{2,14},{14,2},... | collective-permute-start | bytes 12296 | tf_op jit(solution)/shard_map/ppermute | solution.py:389
  27.3 5.4 %collective-permute-start.7 = (f32[8,128]{1,0:T(8,128)S(1)}, f32[8,128]{1,0:T(8,128)S(1)}, u32[]{:S(2)}, u32[]{:S(2)}) collective-permute-start(f32[8,128]{1,0:T(8,128)S(1)} %add.29), channel_id=1, source_target_pairs={{0,64},{16,80},{64,0},{80,16},{32,96},{48,112},{96,32},{112,48},{1... | collective-permute-start | bytes 12296 | tf_op jit(solution)/shard_map/ppermute | solution.py:389
  32.6 6.7 %collective-permute-start.9 = (f32[8,128]{1,0:T(8,128)S(1)}, f32[8,128]{1,0:T(8,128)S(1)}, u32[]{:S(2)}, u32[]{:S(2)}) collective-permute-start(f32[8,128]{1,0:T(8,128)S(1)} %add.30), channel_id=1, source_target_pairs={{0,224},{16,240},{224,0},{240,16},{32,192},{48,208},{192,32},{208,... | collective-permute-start | bytes 12296 | tf_op jit(solution)/shard_map/ppermute | solution.py:389

commit v6 on v5

--- a/solution.py
+++ b/solution.py
@@ -121,7 +121,7 @@
 
 def scenes(rows, cols, heights_in, ids_in, tables, *refs):
     base, (shifted, totals, gains, ups, downs, heights, ids, tall, wide, table, sems) = refs[:8], refs[8:]
-    step, part = 64, TILE // PARTS
+    step, part = 128, TILE // PARTS
     pairs = [(tables, table)]
     for k in range(PARTS):
         at = slice(k * part, k * part + part)

time: 41.1 us -> 40.9 us (level)
  no operation moved by 1% of the time
where the time goes in v6:
time: 40.9 us; the launch traced here: 40.3 us
  starting transfers between devices  21.1 us (52%)
  waiting for transfers between devices  9.71 us (24%)
  Pallas kernels  8.63 us (21%)
  other arithmetic  0.8 us (2%)
    ppermute x5, starting transfers between devices, add(): totals = totals + lax.ppermute(totals, axis, pairs)  16.7 us
    ppermute x5, waiting for transfers between devices, add(): totals = totals + lax.ppermute(totals, axis, pairs)  4.58 us
    ppermute x1, waiting for transfers between devices, local(): even_rows = lax.ppermute(even_rows, ROWS, swaps(rows, 0))  3.2 us
    pallas_call x1, Pallas kernels, local(): pl.pallas_call(lambda *refs: scenes(rows, cols, *refs), out_shape=[jax.Sh...  2.4 us
    pallas_call x1, Pallas kernels, local(): pl.pallas_call(lambda *refs: pyramid(rows, cols, *refs), out_shape=[*stor...  2.28 us
    ppermute x1, starting transfers between devices, local(): odd_cols = lax.ppermute(odd_cols, COLS, swaps(cols, 1))  2.23 us
    pallas_call x1, Pallas kernels, local(): pl.pallas_call(lambda *refs: collapse(rows, cols, *refs), out_shape=tile,...  2.07 us
    ppermute x1, waiting for transfers between devices, local(): even_cols = lax.ppermute(even_cols, COLS, swaps(cols, 0))  1.21 us
  transfers between devices with their start and end apart: 10, of which 6 were waited for; matrix products, arithmetic and copies ran while one was open for 0% of the time, Pallas kernels for 12%

profile of v6, /device:TPU:32, one launch (start us, length us, event | category | flops | bytes accessed | tf_op | source)
XLA Modules:
  0.0 40.3 jit_solution(3307037098139300180)
XLA Ops:
  0.0 0.8 %pad_maximum_fusion.1.refs_2_ = f32[38]{0:T(128)S(1)} fusion(f32[6]{0:T(128)} %param.11, f32[16]{0:T(128)} %param.10, f32[16]{0:T(128)} %param.9), kind=kLoop, calls=%fused_computation.5 | loop fusion | flops 76 | bytes 304 | tf_op jit(solution)/shard_map/concatenate | solution.py:395
  0.8 2.4 %scenes.1 = (f32[560,128]{1,0:T(8,128)S(1)}, f32[560,128]{1,0:T(8,128)S(1)}, f32[560,128]{1,0:T(8,128)S(1)}, f32[560,128]{1,0:T(8,128)S(1)}, f32[560,128]{1,0:T(...) custom-call(f32[512,512]{1,0:T(8,128)} %refs_0_.1, ...), custom_call_target="tpu_custom_call" | custom-call | tf_op jit(solution)/shard_map/scenes/pallas_call | solution.py:396
  3.2 3.1 %collective-permute-start = (f32[8,128]{1,0:T(8,128)S(1)}, f32[8,128]{1,0:T(8,128)S(1)}, u32[]{:S(2)}, u32[]{:S(2)}) collective-permute-start(f32[8,128]{1,0:T(8,128)S(1)} %get-tuple-element.34), channel_id=1, source_target_pairs={{0,3},{3,0},{1,2},{2,1},{4,7},{7,4},{5,6},{6,5},{8,11},{11,8},{9,1... | collective-permute-start | bytes 12296 | tf_op jit(solution)/shard_map/ppermute | solution.py:389
  6.3 2.3 %pyramid.1 = (f32[2,3,304,128]{3,2,1,0:T(8,128)S(1)}, f32[2,2,176,128]{3,2,1,0:T(8,128)S(1)}, f32[2,1,112,128]{3,2,1,0:T(8,128)S(1)}, f32[2,1,80,128]{3,2,1,0:T(...) custom-call(f32[560,128]{1,0:T(8,128)S(1)} %get-tuple-element.35.ref, ...), custom_call_target="tpu_custom_call" | custom-call | tf_op jit(solution)/shard_map/pyramid/pallas_call | solution.py:414
  8.6 0.2 collective-permute-start.1
  8.8 0.7 %collective-permute-start.3 = (f32[8,1152]{1,0:T(8,128)S(1)}, f32[8,1152]{1,0:T(8,128)S(1)}, u32[]{:S(2)}, u32[]{:S(2)}) collective-permute-start(f32[8,1152]{1,0:T(8,128)S(1)} %get-tuple-element.52), channel_id=1, source_target_pairs={{1,2},{2,1},{3,4},{4,3},{5,6},{6,5},{7,8},{8,7},{9,10},{10,9},{11,... | collective-permute-start | bytes 110600 | tf_op jit(solution)/shard_map/ppermute | solution.py:436
  9.5 3.2 %collective-permute-done.1.refs_2_.refs_7_ = f32[8,1280]{1,0:T(8,128)S(1)} collective-permute-done((f32[8,1280]{1,0:T(8,128)S(1)}, f32[8,1280]{1,0:T(8,128)S(1)}, u32[]{:S(2)}, u32[]{:S(2)}) %collective-permute-start.1) | collective-permute-done | bytes 40992 | tf_op jit(solution)/shard_map/ppermute | solution.py:435
  12.7 2.0 %collective-permute-start.2 = (f32[8,128]{1,0:T(8,128)S(1)}, f32[8,128]{1,0:T(8,128)S(1)}, u32[]{:S(2)}, u32[]{:S(2)}) collective-permute-start(f32[8,128]{1,0:T(8,128)S(1)} %slice_add_fusion.2), channel_id=1, source_target_pairs={{0,4},{4,0},{8,12},{12,8},{1,5},{5,1},{9,13},{13,9},{2,6},{6,2},{1... | collective-permute-start | bytes 12296 | tf_op jit(solution)/shard_map/ppermute | solution.py:389
  14.7 0.6 %pack.1 = (f32[80,128]{1,0:T(8,128)S(1)}, f32[80,128]{1,0:T(8,128)S(1)}) custom-call(f32[2,3,304,128]{3,2,1,0:T(8,128)S(1)} %get-tuple-element.44.refs_0_.refs_1_, f32[2,2,176,128]{3,2,1,0:T(8,128)S(1)} %get-tuple-element.45.refs_1_.refs_2_, f32[2,1,112,128]{3,2,1,0:T(8,128)S(1)} %get-tuple-element.46.refs_2_.refs_3_, ...), custom_call_target="tpu_custom_call" | custom-call | tf_op jit(solution)/shard_map/pack/pallas_call | solution.py:426
  15.2 0.0 copy-start.1
  15.3 1.3 %collective-permute-done.2 = f32[8,128]{1,0:T(8,128)S(1)} collective-permute-done((f32[8,128]{1,0:T(8,128)S(1)}, f32[8,128]{1,0:T(8,128)S(1)}, u32[]{:S(2)}, u32[]{:S(2)}) %collective-permute-start.2) | collective-permute-done | bytes 4128 | tf_op jit(solution)/shard_map/ppermute | solution.py:389
  16.5 0.2 edges.1
  16.7 0.1 collective-permute-start.4
  16.8 1.2 %collective-permute-done.4.refs_9_ = f32[88,128]{1,0:T(8,128)S(1)} collective-permute-done((f32[88,128]{1,0:T(8,128)S(1)}, f32[88,128]{1,0:T(8,128)S(1)}, u32[]{:S(2)}, u32[]{:S(2)}) %collective-permute-start.4) | collective-permute-done | bytes 45088 | tf_op jit(solution)/shard_map/ppermute | solution.py:447
  18.0 1.2 %collective-permute-start.5 = (f32[88,128]{1,0:T(8,128)S(1)}, f32[88,128]{1,0:T(8,128)S(1)}, u32[]{:S(2)}, u32[]{:S(2)}) collective-permute-start(f32[88,128]{1,0:T(8,128)S(1)} %broadcast_bitcast_fusion), channel_id=1, source_target_pairs={{0,32},{16,48},{32,0},{48,16},{64,96},{80,112},{96,64},{112,80},{1... | collective-permute-start | bytes 135176 | tf_op jit(solution)/shard_map/ppermute | solution.py:450
  19.2 2.2 %collective-permute-start.8 = (f32[80,128]{1,0:T(8,128)S(1)}, f32[80,128]{1,0:T(8,128)S(1)}, u32[]{:S(2)}, u32[]{:S(2)}) collective-permute-start(f32[80,128]{1,0:T(8,128)S(1)} %get-tuple-element.57), channel_id=1, source_target_pairs={{16,32},{32,16},{48,64},{64,48},{80,96},{96,80},{112,128},{128,112... | collective-permute-start | bytes 122888 | tf_op jit(solution)/shard_map/ppermute | solution.py:452
  21.5 0.7 %collective-permute-done.5 = f32[88,128]{1,0:T(8,128)S(1)} collective-permute-done((f32[88,128]{1,0:T(8,128)S(1)}, f32[88,128]{1,0:T(8,128)S(1)}, u32[]{:S(2)}, u32[]{:S(2)}) %collective-permute-start.5) | collective-permute-done | bytes 45088 | tf_op jit(solution)/shard_map/ppermute | solution.py:450
  22.2 3.3 %collective-permute-start.6 = (f32[8,128]{1,0:T(8,128)S(1)}, f32[8,128]{1,0:T(8,128)S(1)}, u32[]{:S(2)}, u32[]{:S(2)}) collective-permute-start(f32[8,128]{1,0:T(8,128)S(1)} %slice_add_fusion), channel_id=1, source_target_pairs={{0,12},{12,0},{4,8},{8,4},{1,13},{13,1},{5,9},{9,5},{2,14},{14,2},... | collective-permute-start | bytes 12296 | tf_op jit(solution)/shard_map/ppermute | solution.py:389
  25.5 1.6 %collective-permute-done.6 = f32[8,128]{1,0:T(8,128)S(1)} collective-permute-done((f32[8,128]{1,0:T(8,128)S(1)}, f32[8,128]{1,0:T(8,128)S(1)}, u32[]{:S(2)}, u32[]{:S(2)}) %collective-permute-start.6) | collective-permute-done | bytes 4128 | tf_op jit(solution)/shard_map/ppermute | solution.py:389
  27.1 3.3 %collective-permute-start.7 = (f32[8,128]{1,0:T(8,128)S(1)}, f32[8,128]{1,0:T(8,128)S(1)}, u32[]{:S(2)}, u32[]{:S(2)}) collective-permute-start(f32[8,128]{1,0:T(8,128)S(1)} %add.29), channel_id=1, source_target_pairs={{0,64},{16,80},{64,0},{80,16},{32,96},{48,112},{96,32},{112,48},{1... | collective-permute-start | bytes 12296 | tf_op jit(solution)/shard_map/ppermute | solution.py:389
  30.4 2.1 %collapse.1.rest = f32[512,512]{1,0:T(8,128)S(1)} custom-call(f32[8,128]{1,0:T(8,128)S(1)} %get-tuple-element.56.refs_0_, f32[2,3,304,128]{3,2,1,0:T(8,128)S(1)} %get-tuple-element.44.refs_0_.refs_1_, f32[2,2,176,128]{3,2,1,0:T(8,128)S(1)} %get-tuple-element.45.refs_1_.refs_2_, f32[2,1,112,128]{3,2,1,0:T(8,128)S(1)} %get-tuple-element.46.refs_2_.refs_3_, ...), custom_call_target="tpu_custom_call" | custom-call | tf_op jit(solution)/shard_map/collapse/pallas_call | solution.py:453
  32.5 5.0 %collective-permute-start.9 = (f32[8,128]{1,0:T(8,128)S(1)}, f32[8,128]{1,0:T(8,128)S(1)}, u32[]{:S(2)}, u32[]{:S(2)}) collective-permute-start(f32[8,128]{1,0:T(8,128)S(1)} %add.30), channel_id=1, source_target_pairs={{0,224},{16,240},{224,0},{240,16},{32,192},{48,208},{192,32},{208,... | collective-permute-start | bytes 12296 | tf_op jit(solution)/shard_map/ppermute | solution.py:389
  37.4 1.7 %collective-permute-done.9 = f32[8,128]{1,0:T(8,128)S(1)} collective-permute-done((f32[8,128]{1,0:T(8,128)S(1)}, f32[8,128]{1,0:T(8,128)S(1)}, u32[]{:S(2)}, u32[]{:S(2)}) %collective-permute-start.9) | collective-permute-done | bytes 4128 | tf_op jit(solution)/shard_map/ppermute | solution.py:389
  39.2 1.1 %finish.1 = f32[512,512]{1,0:T(8,128)} custom-call(f32[512,512]{1,0:T(8,128)S(1)} %collapse.1.rest, f32[512,128]{1,0:T(8,128)S(1)} %get-tuple-element.60.ups, f32[8,512]{1,0:T(8,128)S(1)} %get-tuple-element.61.downs, f32[8,128]{1,0:T(8,128)S(1)} %add.31.totals), custom_call_target="tpu_custom_call" | custom-call | tf_op jit(solution)/shard_map/finish/pallas_call | solution.py:465
  (17 shorter events, 0.1 us)
Async XLA Ops:
  3.2 5.4 %collective-permute-start = (f32[8,128]{1,0:T(8,128)S(1)}, f32[8,128]{1,0:T(8,128)S(1)}, u32[]{:S(2)}, u32[]{:S(2)}) collective-permute-start(f32[8,128]{1,0:T(8,128)S(1)} %get-tuple-element.34), channel_id=1, source_target_pairs={{0,3},{3,0},{1,2},{2,1},{4,7},{7,4},{5,6},{6,5},{8,11},{11,8},{9,1... | collective-permute-start | bytes 12296 | tf_op jit(solution)/shard_map/ppermute | solution.py:389
  8.6 4.1 %collective-permute-start.1 = (f32[8,1280]{1,0:T(8,128)S(1)}, f32[8,1280]{1,0:T(8,128)S(1)}, u32[]{:S(2)}, u32[]{:S(2)}) collective-permute-start(f32[8,1280]{1,0:T(8,128)S(1)} %pad_maximum_fusion), channel_id=1, source_target_pairs={{0,1},{1,0},{2,3},{3,2},{4,5},{5,4},{6,7},{7,6},{8,9},{9,8},{10,11... | collective-permute-start | bytes 122888 | tf_op jit(solution)/shard_map/ppermute | solution.py:435
  8.8 7.7 %collective-permute-start.3 = (f32[8,1152]{1,0:T(8,128)S(1)}, f32[8,1152]{1,0:T(8,128)S(1)}, u32[]{:S(2)}, u32[]{:S(2)}) collective-permute-start(f32[8,1152]{1,0:T(8,128)S(1)} %get-tuple-element.52), channel_id=1, source_target_pairs={{1,2},{2,1},{3,4},{4,3},{5,6},{6,5},{7,8},{8,7},{9,10},{10,9},{11,... | collective-permute-start | bytes 110600 | tf_op jit(solution)/shard_map/ppermute | solution.py:436
  12.7 3.8 %collective-permute-start.2 = (f32[8,128]{1,0:T(8,128)S(1)}, f32[8,128]{1,0:T(8,128)S(1)}, u32[]{:S(2)}, u32[]{:S(2)}) collective-permute-start(f32[8,128]{1,0:T(8,128)S(1)} %slice_add_fusion.2), channel_id=1, source_target_pairs={{0,4},{4,0},{8,12},{12,8},{1,5},{5,1},{9,13},{13,9},{2,6},{6,2},{1... | collective-permute-start | bytes 12296 | tf_op jit(solution)/shard_map/ppermute | solution.py:389
  14.7 15.7 %copy-start = (bf16[384,512]{1,0:T(8,128)(2,1)S(1)}, bf16[384,512]{1,0:T(8,128)(2,1)}, u32[]{:S(2)}) copy-start(bf16[384,512]{1,0:T(8,128)(2,1)} %constant.5.clone.refs_12_) | copy-start | bytes 1179652
  15.2 15.1 %copy-start.1 = (bf16[256,384]{1,0:T(8,128)(2,1)S(1)}, bf16[256,384]{1,0:T(8,128)(2,1)}, u32[]{:S(2)}) copy-start(bf16[256,384]{1,0:T(8,128)(2,1)} %constant.4.clone.refs_11_) | copy-start | bytes 589828
  16.7 1.3 %collective-permute-start.4 = (f32[88,128]{1,0:T(8,128)S(1)}, f32[88,128]{1,0:T(8,128)S(1)}, u32[]{:S(2)}, u32[]{:S(2)}) collective-permute-start(f32[88,128]{1,0:T(8,128)S(1)} %get-tuple-element.53), channel_id=1, source_target_pairs={{0,16},{16,0},{32,48},{48,32},{64,80},{80,64},{96,112},{112,96},{1... | collective-permute-start | bytes 135176 | tf_op jit(solution)/shard_map/ppermute | solution.py:447
  18.0 4.1 %collective-permute-start.5 = (f32[88,128]{1,0:T(8,128)S(1)}, f32[88,128]{1,0:T(8,128)S(1)}, u32[]{:S(2)}, u32[]{:S(2)}) collective-permute-start(f32[88,128]{1,0:T(8,128)S(1)} %broadcast_bitcast_fusion), channel_id=1, source_target_pairs={{0,32},{16,48},{32,0},{48,16},{64,96},{80,112},{96,64},{112,80},{1... | collective-permute-start | bytes 135176 | tf_op jit(solution)/shard_map/ppermute | solution.py:450
  19.2 11.1 %collective-permute-start.8 = (f32[80,128]{1,0:T(8,128)S(1)}, f32[80,128]{1,0:T(8,128)S(1)}, u32[]{:S(2)}, u32[]{:S(2)}) collective-permute-start(f32[80,128]{1,0:T(8,128)S(1)} %get-tuple-element.57), channel_id=1, source_target_pairs={{16,32},{32,16},{48,64},{64,48},{80,96},{96,80},{112,128},{128,112... | collective-permute-start | bytes 122888 | tf_op jit(solution)/shard_map/ppermute | solution.py:452
  22.2 4.9 %collective-permute-start.6 = (f32[8,128]{1,0:T(8,128)S(1)}, f32[8,128]{1,0:T(8,128)S(1)}, u32[]{:S(2)}, u32[]{:S(2)}) collective-permute-start(f32[8,128]{1,0:T(8,128)S(1)} %slice_add_fusion), channel_id=1, source_target_pairs={{0,12},{12,0},{4,8},{8,4},{1,13},{13,1},{5,9},{9,5},{2,14},{14,2},... | collective-permute-start | bytes 12296 | tf_op jit(solution)/shard_map/ppermute | solution.py:389
  27.1 5.4 %collective-permute-start.7 = (f32[8,128]{1,0:T(8,128)S(1)}, f32[8,128]{1,0:T(8,128)S(1)}, u32[]{:S(2)}, u32[]{:S(2)}) collective-permute-start(f32[8,128]{1,0:T(8,128)S(1)} %add.29), channel_id=1, source_target_pairs={{0,64},{16,80},{64,0},{80,16},{32,96},{48,112},{96,32},{112,48},{1... | collective-permute-start | bytes 12296 | tf_op jit(solution)/shard_map/ppermute | solution.py:389
  32.5 6.7 %collective-permute-start.9 = (f32[8,128]{1,0:T(8,128)S(1)}, f32[8,128]{1,0:T(8,128)S(1)}, u32[]{:S(2)}, u32[]{:S(2)}) collective-permute-start(f32[8,128]{1,0:T(8,128)S(1)} %add.30), channel_id=1, source_target_pairs={{0,224},{16,240},{224,0},{240,16},{32,192},{48,208},{192,32},{208,... | collective-permute-start | bytes 12296 | tf_op jit(solution)/shard_map/ppermute | solution.py:389
